TPU v7x, 512 devices: a whole 4x4x16 slice. The times are simulated.
512 devices in a mesh: dp: 64 (over z, y), space: 8 (over x, core).
Axes of the slice: x: 4, y: 4, z: 16, core: 2. Of those that a mesh axis runs over, the one named last changes fastest.
Arguments:
- volume: bfloat16 [64, 4, 64, 8, 128], P('dp', None, 'space'), may hold values from -6 to 6
- w_first: bfloat16 [32, 4, 3, 3, 3], replicated, may hold values from -0.625 to 0.625
- b_first: float32 [32], replicated, may hold values from -0.5 to 0.5
- w_second: bfloat16 [64, 32, 3, 3, 3], replicated, may hold values from -0.21875 to 0.21875
- b_second: float32 [64], replicated, may hold values from -0.5 to 0.5
- cotangent: bfloat16 [64, 64, 16, 2, 32], P('dp', None, 'space'), may hold values from -1 to 1
Outputs:
- features: bfloat16 [64, 64, 16, 2, 32], P('dp', None, 'space')
- grad_w_first: float32 [32, 4, 3, 3, 3], replicated
- grad_b_first: float32 [32], replicated
- grad_w_second: float32 [64, 32, 3, 3, 3], replicated
- grad_b_second: float32 [64], replicated
All inputs are finite; a program needn't handle non-finite values.
Results may differ from a plain program's by a relative error of at most 0.005.
The roundings to bfloat16 on the way count: a program that leaves them out, or rounds other values in their place, can miss the bound.
Values may be sent and summed in bfloat16 or wider, within the bound.
No kernel may reach another device: no remote copies, remote signals or barrier semaphores. Data moves between devices by JAX's collectives and lax.ppermute only.
A program may use at most 128 MiB of HBM per device.

v0:
```python
import jax
import jax.numpy as jnp
from jax import lax
from jax.sharding import PartitionSpec as P


def extended(array, sides, width):
    for axis, dim in sides:
        count, length = (lax.axis_size(axis), array.shape[dim])
        up = [(i, (i + 1) % count) for i in range(count - 1)]
        down = [(j, i) for i, j in up]
        last = lax.slice_in_dim(array, length - width, length, axis=dim)
        initial = lax.slice_in_dim(array, 0, width, axis=dim)
        before = lax.ppermute(last, axis, up)
        after = lax.ppermute(initial, axis, down)
        array = jnp.concatenate([before, array, after], axis=dim)
    return array


def conv_valid(padded, weights):
    return lax.conv_general_dilated(
        padded[None],
        weights,
        (1, 1, 1),
        "VALID",
        dimension_numbers=("NCDHW", "OIDHW", "NCDHW"),
        preferred_element_type=jnp.float32,
    )[0]


def weight_grad(padded, upstream):
    result = lax.conv_general_dilated(
        padded[None],
        upstream[None],
        (1, 1, 1),
        "VALID",
        dimension_numbers=("CNDHW", "IODHW", "NCDHW"),
        preferred_element_type=jnp.float32,
    )
    return jnp.transpose(result, (1, 0, 2, 3, 4))


def flip_weights(weights):
    return jnp.flip(jnp.transpose(weights, (1, 0, 2, 3, 4)), axis=(2, 3, 4))


def pool_cells(values):
    shape = values.shape
    blocks = values.reshape(shape[0], shape[1] // 2, 2, shape[2] // 2, 2, shape[3] // 2, 2)
    return jnp.mean(blocks, axis=(2, 4, 6))


def squash(values):
    return pool_cells(jnp.where(values > 0.0, values, 0.3 * values))


def pad_sides(values):
    return jnp.pad(values, ((0, 0), (0, 0), (1, 1), (1, 1)))


def local(volume, w_first, b_first, w_second, b_second, cotangent):
    local_volume = volume[0]
    flipped = flip_weights(w_second)
    padded_in = pad_sides(extended(local_volume, (("space", 1),), 1))
    pre_first = conv_valid(padded_in, w_first) + b_first[:, None, None, None]
    act_float, back_first = jax.vjp(squash, pre_first)
    act_first = act_float.astype(jnp.bfloat16)
    padded_act = pad_sides(extended(act_first, (("space", 1),), 1))
    pre_second = conv_valid(padded_act, w_second) + b_second[:, None, None, None]
    pooled, back_second = jax.vjp(squash, pre_second)
    grad_second = back_second(cotangent[0].astype(jnp.float32))[0].astype(jnp.bfloat16)
    grad_w_second = weight_grad(padded_act, grad_second)
    grad_b_second = jnp.sum(grad_second, axis=(1, 2, 3), dtype=jnp.float32)
    padded_grad = pad_sides(extended(grad_second, (("space", 1),), 1))
    grad_act = conv_valid(padded_grad, flipped)
    grad_first = back_first(grad_act)[0].astype(jnp.bfloat16)
    grad_w_first = weight_grad(padded_in, grad_first)
    grad_b_first = jnp.sum(grad_first, axis=(1, 2, 3), dtype=jnp.float32)
    grad_w_first, grad_b_first, grad_w_second, grad_b_second = lax.psum(
        (grad_w_first, grad_b_first, grad_w_second, grad_b_second), ("dp", "space")
    )
    return (
        pooled.astype(jnp.bfloat16)[None],
        grad_w_first,
        grad_b_first,
        grad_w_second,
        grad_b_second,
    )


def solution(mesh):
    placed = (
        P("dp", None, "space", None, None),
        P(),
        P(),
        P(),
        P(),
        P("dp", None, "space", None, None),
    )
    return jax.shard_map(
        local,
        mesh=mesh,
        in_specs=placed,
        out_specs=(P("dp", None, "space", None, None), P(), P(), P(), P()),
        check_vma=False,
    )
```

profile of v0, /device:TPU:1, one launch (start us, length us, event | category | flops | bytes accessed | tf_op | source)
XLA Modules:
  0.0 548.2 jit_solution(15997308138618044224)
XLA Ops:
  7.2 0.8 fusion.62
  8.0 4.5 collective-permute-start
  12.5 5.6 %collective-permute-start.1 = (bf16[4,1,8,128]{3,2,1,0:T(8,128)(2,1)S(1)}, bf16[4,1,8,128]{3,2,1,0:T(8,128)(2,1)S(1)}, u32[]{:S(2)}, u32[]{:S(2)}) collective-permute-start(bf16[4,1,8,128]{3,2,1,0:T(8,128)(2,1)S(1)} %get-tuple-element.37), channel_id=1, source_target_pairs={{1,0},{2,1},{3,2},{4,3},{5,4},{6,5},{7,6},{9,8},{10,9},{11,10},{12... | collective-permute-start | bytes 24584 | tf_op jit(solution)/shard_map/ppermute | solution.py:15
  18.1 0.8 multiply_bitcast_fusion
  18.9 1.0 fusion.64
  20.0 0.6 reshape.103
  20.7 2.9 copy.96
  23.6 0.2 slice.34
  23.8 9.9 %add_compare_fusion = (pred[8,8,8,17,32]{4,2,3,1,0:T(8,128)(4,1)S(1)}, f32[8,8,8,17,32]{4,2,3,1,0:T(8,128)S(1)}) fusion(f32[32]{0:T(128)S(1)} %copy-done.4, bf16[32,4,3,3,3]{0,1,4,3,2:T(4,128)(2,1)S(1)} %copy-done.5, bf16[4,10,10,1,7,2]{4,0,5,2,1,3:T(4,128)(2,1)S(1)} %slice.34, bf16[4,10,10,1,8,17]{4,0,5,2,1,3:T(4,128)(2,1)S(1)} %copy.96, ...), kind=kOutput, calls=%fused_computation.1 | convolution fusion | flops 61362432 | bytes 1519816 | tf_op jit(solution)/shard_map/conv_general_dilated | solution.py:21
  33.7 0.8 copy.97
  34.5 0.3 slice.35
  34.8 5.1 fusion
  39.9 0.1 multiply_convert_fusion
  40.1 1.9 collective-permute-start.2
  42.0 2.4 collective-permute-start.3
  44.4 0.2 fusion.63
  44.7 0.5 copy.102
  45.3 1.8 copy.124
  47.1 20.6 %copy.111 = bf16[1,4,10,10,130]{1,0,4,3,2:T(2,128)(2,1)} copy(bf16[1,4,10,10,130]{4,3,2,1,0:T(8,128)(2,1)S(1)} %fusion.63) | data formatting | bytes 208000 | tf_op jit(solution)/shard_map/broadcast_in_dim | solution.py:22
  67.7 0.5 fusion.66
  68.2 0.2 pad.17
  68.5 0.1 copy.99
  68.6 0.2 copy-done.3
  68.9 1.4 add_compare_fusion.1
  70.4 0.1 copy.114
  70.5 0.1 broadcast_in_dim.28
  70.7 0.9 convert_reduce_fusion.1
  71.5 0.5 fusion.65
  72.0 7.4 %fusion.17 = f32[64,32,3,3,3]{0,1,4,3,2:T(8,128)} fusion(bf16[1,32,6,6,66]{1,3,4,2,0:T(8,128)(2,1)S(1)} %fusion.65, bf16[1,64,4,4,64]{1,3,4,2,0:T(4,128)(2,1)S(1)} %get-tuple-element.29), kind=kOutput, calls=%fused_computation.33 | convolution fusion | flops 113246208 | bytes 504320 | tf_op jit(solution)/shard_map/transpose | solution.py:40
  79.5 0.2 copy.100
  79.7 0.3 add_convert_fusion.2
  79.9 0.6 fusion.43
  80.6 3.2 collective-permute-start.4
  83.8 2.1 collective-permute-start.5
  86.0 0.6 copy.117
  86.6 2.8 collective-permute-done.5
  89.4 0.5 fusion.28
  89.9 0.2 pad.19
  90.2 2.2 fusion.16
  92.4 0.2 copy.107
  92.7 4.1 broadcast_in_dim.30
  96.8 3.1 copy.109
  99.9 0.4 convert_reduce_fusion
  100.3 4.8 copy.112
  105.1 50.2 %fusion.67 = f32[32,4,3,3,3]{0,1,4,3,2:T(4,128)S(1)} fusion(bf16[1,4,10,10,130]{1,0,4,3,2:T(2,128)(2,1)} %copy.111, bf16[1,32,8,8,128]{1,0,4,3,2:T(2,128)(2,1)} %copy.112), kind=kOutput, calls=%fused_computation.103 | convolution fusion | flops 56623104 | bytes 642112 | tf_op jit(solution)/shard_map/transpose | solution.py:40
  155.3 109.1 %all-reduce.3 = (f32[32,4,3,3,3]{0,1,4,3,2:T(4,128)}, f32[32]{0:T(128)}, f32[64]{0:T(128)}) all-reduce(f32[32,4,3,3,3]{0,1,4,3,2:T(4,128)S(1)} %fusion.67, f32[32]{0:T(128)S(1)} %get-tuple-element.30, f32[64]{0:T(128)S(1)} %copy-done.2), channel_id=1, replica_groups=mesh['dp'=64,'space'=8] {'dp','space'}, use_global_device_ids=true, to_apply=%region_2.3 | all-reduce | flops 3552 | bytes 28416 | tf_op jit(solution)/shard_map/psum | solution.py:79
  264.4 274.7 %all-reduce.6.cloned.1.call-done = f32[64,32,3,3,3]{0,1,4,3,2:T(8,128)} async-done(((f32[64,32,3,3,3]{0,1,4,3,2:T(8,128)}), f32[64,32,3,3,3]{0,1,4,3,2:T(8,128)}) %all-reduce.6.cloned.1.call-update) | async-done | bytes 221200 | tf_op jit(solution)/shard_map/psum | solution.py:79
  539.2 1.8 copy.130
  (34 shorter events, 0.8 us)
Async XLA Ops:
  7.2 61.5 %copy-start = (bf16[64,32,3,3,3]{0,1,4,3,2:T(8,128)(2,1)S(1)}, bf16[64,32,3,3,3]{0,1,4,3,2:T(8,128)(2,1)}, u32[]{:S(2)}) copy-start(bf16[64,32,3,3,3]{0,1,4,3,2:T(8,128)(2,1)} %param.9) | copy-start | bytes 331780
  7.2 532.0 %all-reduce.6.cloned.1.call-start = ((), (), s32[]{:S(2)}) async-start(), calls=%async_computation | async-start | bytes 884736 | tf_op jit(solution)/shard_map/psum | solution.py:79
  8.0 10.9 %collective-permute-start = (bf16[4,1,8,128]{3,2,1,0:T(8,128)(2,1)S(1)}, bf16[4,1,8,128]{3,2,1,0:T(8,128)(2,1)S(1)}, u32[]{:S(2)}, u32[]{:S(2)}) collective-permute-start(bf16[4,1,8,128]{3,2,1,0:T(8,128)(2,1)S(1)} %get-tuple-element.36), channel_id=1, source_target_pairs={{0,1},{1,2},{2,3},{3,4},{4,5},{5,6},{6,7},{8,9},{9,10},{10,11},{11... | collective-permute-start | bytes 24584 | tf_op jit(solution)/shard_map/ppermute | solution.py:14
  12.5 6.4 %collective-permute-start.1 = (bf16[4,1,8,128]{3,2,1,0:T(8,128)(2,1)S(1)}, bf16[4,1,8,128]{3,2,1,0:T(8,128)(2,1)S(1)}, u32[]{:S(2)}, u32[]{:S(2)}) collective-permute-start(bf16[4,1,8,128]{3,2,1,0:T(8,128)(2,1)S(1)} %get-tuple-element.37), channel_id=1, source_target_pairs={{1,0},{2,1},{3,2},{4,3},{5,4},{6,5},{7,6},{9,8},{10,9},{11,10},{12... | collective-permute-start | bytes 24584 | tf_op jit(solution)/shard_map/ppermute | solution.py:15
  20.7 3.1 copy-start.4
  20.7 3.1 copy-start.5
  20.7 3.1 copy-start.6
  34.8 9.7 %copy-start.1 = (bf16[1,4,8,8,128]{4,3,2,1,0:T(8,128)(2,1)S(1)}, bf16[1,4,8,8,128]{4,3,2,1,0:T(8,128)(2,1)}, u32[]{:S(2)}) copy-start(bf16[1,4,8,8,128]{4,3,2,1,0:T(8,128)(2,1)} %param.6) | copy-start | bytes 196612
  40.1 27.6 %collective-permute-start.2 = (bf16[32,1,4,64]{0,2,3,1:T(4,128)(2,1)S(1)}, bf16[32,1,4,64]{0,2,3,1:T(4,128)(2,1)S(1)}, u32[]{:S(2)}, u32[]{:S(2)}) collective-permute-start(bf16[32,1,4,64]{0,2,3,1:T(4,128)(2,1)S(1)} %get-tuple-element.34), channel_id=1, source_target_pairs={{0,1},{1,2},{2,3},{3,4},{4,5},{5,6},{6,7},{8,9},{9,10},{10,11},{11... | collective-permute-start | bytes 49160 | tf_op jit(solution)/shard_map/ppermute | solution.py:14
  42.0 25.7 %collective-permute-start.3 = (bf16[32,1,4,64]{0,2,3,1:T(4,128)(2,1)S(1)}, bf16[32,1,4,64]{0,2,3,1:T(4,128)(2,1)S(1)}, u32[]{:S(2)}, u32[]{:S(2)}) collective-permute-start(bf16[32,1,4,64]{0,2,3,1:T(4,128)(2,1)S(1)} %get-tuple-element.35), channel_id=1, source_target_pairs={{1,0},{2,1},{3,2},{4,3},{5,4},{6,5},{7,6},{9,8},{10,9},{11,10},{12... | collective-permute-start | bytes 49160 | tf_op jit(solution)/shard_map/ppermute | solution.py:15
  68.2 0.7 copy-start.3
  68.2 0.7 copy-start.7
  80.6 6.0 %collective-permute-start.4 = (bf16[64,1,4,64]{0,2,3,1:T(4,128)(2,1)S(1)}, bf16[64,1,4,64]{0,2,3,1:T(4,128)(2,1)S(1)}, u32[]{:S(2)}, u32[]{:S(2)}) collective-permute-start(bf16[64,1,4,64]{0,2,3,1:T(4,128)(2,1)S(1)} %get-tuple-element.32), channel_id=1, source_target_pairs={{0,1},{1,2},{2,3},{3,4},{4,5},{5,6},{6,7},{8,9},{9,10},{10,11},{11... | collective-permute-start | bytes 98312 | tf_op jit(solution)/shard_map/ppermute | solution.py:14
  83.8 5.6 %collective-permute-start.5 = (bf16[64,1,4,64]{0,2,3,1:T(4,128)(2,1)S(1)}, bf16[64,1,4,64]{0,2,3,1:T(4,128)(2,1)S(1)}, u32[]{:S(2)}, u32[]{:S(2)}) collective-permute-start(bf16[64,1,4,64]{0,2,3,1:T(4,128)(2,1)S(1)} %get-tuple-element.33), channel_id=1, source_target_pairs={{1,0},{2,1},{3,2},{4,3},{5,4},{6,5},{7,6},{9,8},{10,9},{11,10},{12... | collective-permute-start | bytes 98312 | tf_op jit(solution)/shard_map/ppermute | solution.py:15
  105.1 50.2 %copy-start.2 = (f32[64]{0:T(128)S(1)}, f32[64]{0:T(128)}, u32[]{:S(2)}) copy-start(f32[64]{0:T(128)} %get-tuple-element.28) | copy-start | bytes 772
Sparse Core Ops, SparseCore 0:
  79.6 459.5 all-reduce.5
where the time goes:
time: 559 us; the launch traced here: 548 us
  waiting for transfers between devices  278 us (50%)
  blocking collectives  109 us (19%)
  matrix products  71.1 us (13%)
  local copies, waits for them, and re-layouts  44.9 us (8%)
  starting transfers between devices  19.7 us (4%)
  between operations  14.8 us (3%)
  other arithmetic  11 us (2%)
    psum x1, waiting for transfers between devices, local(): lax.psum((grad_w_first, grad_b_first, grad_w_second, grad_b_second), ('dp...  275 us
    psum x1, blocking collectives, local(): lax.psum((grad_w_first, grad_b_first, grad_w_second, grad_b_second), ('dp...  109 us
    transpose x2, matrix products, weight_grad(): return jnp.transpose(result, (1, 0, 2, 3, 4))  57.6 us
    broadcast_in_dim x4, local copies, waits for them, and re-layouts, conv_valid(): padded[None]  21.2 us
    conv_general_dilated x3, matrix products, conv_valid(): lax.conv_general_dilated(padded[None], weights, (1, 1, 1), 'VALID', dimen...  13.5 us
  transfers between devices with their start and end apart: 7, of which 2 were waited for; matrix products, arithmetic and copies ran while one was open for 17% of the time, Pallas kernels for 0%

commit v1 on v0

v1 whole, which is shorter than its diff:
```python
import jax
import jax.numpy as jnp
from jax import lax
from jax.experimental import pallas as pl
from jax.experimental.pallas import tpu as pltpu
from jax.sharding import Mesh, PartitionSpec as P

BF16, F32 = jnp.bfloat16, jnp.float32
VMEM = pl.BlockSpec(memory_space=pltpu.VMEM)
PARAMS = pltpu.CompilerParams(vmem_limit_bytes=48 * 1024 * 1024)
C_IN, C_MID, C_OUT, Y, X = 4, 32, 64, 8, 128
DEEP = 5
COT_AT = C_IN * DEEP
ONES_AT = COT_AT + 4
BLOCKS = ONES_AT + 1
ROWS_W2, ROWS_W1, ROWS_B2, ROWS_B1, ROWS = 0, 432, 472, 480, 512


def dot(a, b, dims=((1,), (0,))):
    return lax.dot_general(a, b, (dims, ((), ())), preferred_element_type=F32)


def iota(shape, dim):
    return lax.broadcasted_iota(jnp.int32, shape, dim)


def split(v):
    hi = v.astype(BF16)
    return hi, (v - hi.astype(F32)).astype(BF16)


def leaky(v):
    return jnp.where(v > 0.0, v, 0.3 * v)


def rolled(v, shift):
    return pltpu.roll(v, shift, 1)


def taps(v, period):
    place = iota(v.shape, 1) % period
    before = jnp.where(place == 0, 0.0, rolled(v, 1))
    after = jnp.where(place == period - 1, 0.0, rolled(v, v.shape[1] - 1))
    return before, v, after


def pack_kernel(vol, cot, up, down):
    for c in range(C_IN):
        up[c * DEEP : (c + 1) * DEEP] = vol[c, 8 - DEEP :]
        down[c * DEEP : (c + 1) * DEEP] = vol[c, :DEEP]
    for ref, d in ((up, 1), (down, 0)):
        both = jnp.concatenate([cot[d, 0].astype(F32), cot[d, 1].astype(F32)], axis=1)
        ref[COT_AT:ONES_AT] = both.reshape(4, 8, 128).astype(BF16)
        ref[ONES_AT] = jnp.ones((8, 128), BF16)


def bias_rows(bias, copies):
    hi = bias.astype(BF16).astype(F32)
    lo = (bias - hi).astype(BF16).astype(F32)
    rest = bias - hi - lo
    hi, lo, rest = (jnp.concatenate([v] * copies, axis=1) for v in (hi, lo, rest))
    row = iota((128, 256), 0)
    zero = jnp.zeros((128, 256), F32)
    return jnp.where(row == 0, hi, jnp.where(row == 1, lo, jnp.where(row == 2, rest, zero)))


def weights_kernel(w1, b1, w2, b2, t1, t2, t2g):
    wide = jnp.concatenate([w1[...]] * 4, axis=1)
    y_in = iota((8, 128), 0)
    lanes = iota((8, 128), 1) // C_MID
    blocks = []
    for kd in range(3):
        for kx in range(3):
            for c in range(C_IN):
                halves = []
                for half in range(2):
                    ky = y_in - (lanes + 4 * half) + 1
                    total = jnp.zeros((8, 128), F32)
                    for k in range(3):
                        at = ((kd * 3 + k) * 3 + kx) * C_IN + c
                        total = jnp.where(ky == k, wide[at : at + 1], total)
                    halves.append(total)
                blocks.append(jnp.concatenate(halves, axis=1))
    body = jnp.concatenate(blocks + [bias_rows(b1[...], 8)[:96]], axis=0)
    t1[...] = body.T.astype(BF16)
    nothing = jnp.zeros((C_MID, C_OUT), F32)
    for kd in range(3):
        for kx in range(3):
            w = [w2[(kd * 3 + ky) * 3 + kx].astype(F32) for ky in range(3)]
            pair = {
                a: jnp.concatenate([w[a] if a < 3 else nothing, w[a - 1] if a > 0 else nothing], axis=1)
                for a in range(4)
            }
            none = jnp.zeros((C_MID, 128), F32)
            block = jnp.concatenate(
                [
                    jnp.concatenate([pair.get(y - 2 * p + 1, none) for p in range(2)], axis=1)
                    for y in range(4)
                ],
                axis=0,
            )
            t2g[kd * 128 : (kd + 1) * 128, kx * 256 : (kx + 1) * 256] = block.astype(BF16)
            at = (kd * 3 + kx) * 128
            t2[:, at : at + 128] = block.T.astype(BF16)
    t2[:, 1152:] = bias_rows(b2[...], 4).T.astype(BF16)


def main_kernel(vol, before, behind, cot, t1, t2, t2g, feat, grads, p1, pre1, p2, g4x, g1):
    lane = iota((1, 128), 1)
    low = lane < 64

    for z in range(-5, 13):
        def plane(c):
            if z < 0:
                return before[c * DEEP + z + 5]
            if z >= 8:
                return behind[c * DEEP + z - 8]
            return vol[c, z]
        v = jnp.concatenate([plane(c).astype(F32) for c in range(C_IN)], axis=0)
        stack = jnp.concatenate(taps(v, 128), axis=0).astype(BF16)
        for kd in range(3):
            to = z - kd + 1 + 4
            if 0 <= to < 16:
                p1[kd * 96 : (kd + 1) * 96, to * 128 : (to + 1) * 128] = stack
    p1[288:, :] = jnp.ones((96, 2048), BF16)

    his, los = [], []
    for d in range(8):
        pre = dot(t1[...], p1[:, d * 256 : (d + 1) * 256])
        if 2 <= d < 6:
            pre1[:, (d - 2) * 256 : (d - 1) * 256] = pre
        act = leaky(pre).reshape(4, 2, C_MID, 256)
        act = (act[:, 0] + act[:, 1]).reshape(128, 256)
        hi, lo = split(act[:, :128] + act[:, 128:])
        his.append(hi)
        los.append(lo)

    row, col = iota((256, 128), 0), iota((256, 128), 1)
    pool = jnp.where((row // 128 == col // 64) & (row % 128 // 2 == col % 64), 0.125, 0.0).astype(BF16)
    m_before = before[ONES_AT].astype(F32)[:1]
    m_behind = behind[ONES_AT].astype(F32)[:1]
    for r in range(6):
        act = dot(jnp.concatenate([his[r], his[r + 2]], axis=1), pool)
        act = act + dot(jnp.concatenate([los[r], los[r + 2]], axis=1), pool)
        if r < 2:
            act = act * jnp.where(low, m_before, 1.0)
        if r >= 4:
            act = act * jnp.where(low, 1.0, m_behind)
        act = act.astype(BF16).astype(F32)
        stack = jnp.concatenate(taps(act, 64), axis=0).astype(BF16)
        for kd in range(3):
            to = r - kd
            if 0 <= to < 4:
                p2[kd * 384 : (kd + 1) * 384, to * 128 : (to + 1) * 128] = stack
    p2[1152:, :] = jnp.ones((128, 512), BF16)

    pre2 = dot(t2[...], p2[...])

    act = leaky(pre2[:, 128:384]).reshape(2, 2, C_OUT, 256)
    act = act[:, 0] + act[:, 1]
    act = act[:, :, :128] + act[:, :, 128:]
    row, col = iota((64, 128), 0), iota((64, 128), 1)
    pool = jnp.where((row // 32 == col // 64) & (row % 32 == col % 64 // 2), 0.125, 0.0).astype(BF16)
    for y in range(2):
        hi, lo = split(act[y])
        out = dot(pool, hi, ((1,), (1,))) + dot(pool, lo, ((1,), (1,)))
        for d in range(2):
            feat[d, y] = out[d * 32 : (d + 1) * 32].astype(BF16)

    pieces = [before[COT_AT:ONES_AT].astype(F32).reshape(32, 128)]
    for d in range(2):
        pieces.append(jnp.concatenate([cot[d, 0].astype(F32), cot[d, 1].astype(F32)], axis=1))
    pieces.append(behind[COT_AT:ONES_AT].astype(F32).reshape(32, 128))
    cots = jnp.concatenate(pieces, axis=0).T.astype(BF16)
    row, col = iota((128, 384), 0), iota((128, 384), 1)
    spread = jnp.where((row // 32 == col // 128 + col % 128 // 64) & (row % 32 == col % 64 // 2), 0.125, 0.0)
    up = dot(cots, spread.astype(BF16))
    up = jnp.concatenate([up[:, :256], up[:, 128:]], axis=1).reshape(2, 1, C_OUT, 512)
    mask = pre2.reshape(2, 2, C_OUT, 512) > 0.0
    grad = jnp.where(mask, up, 0.3 * up).reshape(256, 512).astype(BF16)
    for r in range(4):
        piece = grad[:, r * 128 : (r + 1) * 128].astype(F32)
        for kx, tap in enumerate(reversed(taps(piece, 64))):
            g4x[kx * 256 : (kx + 1) * 256, r * 128 : (r + 1) * 128] = tap.astype(BF16)

    back = dot(t2g[0:128], g4x[:, 256:512])
    back = back + dot(t2g[128:256], g4x[:, 128:384])
    back = back + dot(t2g[256:384], g4x[:, 0:256])
    one = back * 0.125
    less = 0.3 * one
    stack = jnp.concatenate([one[:, :128], one[:, 128:], less[:, :128], less[:, 128:]], axis=0)
    row, col = iota((128, 256), 0), iota((128, 256), 1)
    spread = jnp.where(row == col // 128 * 64 + col % 128 // 2, 1.0, 0.0).astype(BF16)
    wide = dot(stack.astype(BF16), spread)
    for z in range(8):
        a = z // 2
        at, half = (a % 2) * 128, (a // 2) * 128
        yes = wide[at : at + 128, half : half + 128].reshape(4, 1, C_MID, 128)
        no = wide[256 + at : 384 + at, half : half + 128].reshape(4, 1, C_MID, 128)
        mask = pre1[:, z * 128 : (z + 1) * 128].reshape(4, 2, C_MID, 128) > 0.0
        g1[:, z * 128 : (z + 1) * 128] = jnp.where(mask, yes, no).reshape(256, 128).astype(BF16)

    d2 = dot(p2[0:1168, 128:384], g4x[256:512, 128:384], ((1,), (1,)))
    for kd in range(3):
        for kx in range(3):
            base = (kd * 3 + kx) * 128
            def block(y, p):
                return d2[base + y * 32 : base + (y + 1) * 32, p * 128 : (p + 1) * 128]
            for ky in range(3):
                even = [block(y, p) for p in range(2) for y in [2 * p + ky - 1] if 0 <= y < 4]
                odd = [block(y, p) for p in range(2) for y in [2 * p + ky] if 0 <= y < 4]
                total = sum(even[1:], even[0]) + rolled(sum(odd[1:], odd[0]), 64)
                at = ROWS_W2 + ((kd * 3 + ky) * 3 + kx) * 16
                grads[at : at + 16] = jnp.where(low, total[:16], rolled(total[16:], 64))
    d = d2[1152:1160, :128] + d2[1152:1160, 128:]
    grads[ROWS_B2 : ROWS_B2 + 8] = d + rolled(d, 64)

    d1 = dot(p1[0:304, 512:1536], g1[...], ((1,), (1,)))
    body = d1[:288].reshape(36, 8, 256)
    ky = iota((1, 8, 256), 1) - iota((1, 8, 256), 2) // C_MID + 1
    total = jnp.zeros((36, 128), F32)
    for k in range(3):
        part = jnp.sum(jnp.where(ky == k, body, 0.0), axis=1)
        part = part[:, :128] + part[:, 128:]
        part = part + rolled(part, 64)
        part = part + rolled(part, 32)
        total = jnp.where(lane // 32 == k, part, total)
    grads[ROWS_W1 : ROWS_W1 + 40] = jnp.concatenate([total, jnp.zeros((4, 128), F32)], axis=0)
    d = d1[288:296, :128] + d1[288:296, 128:]
    d = d + rolled(d, 64)
    grads[ROWS_B1 : ROWS_B1 + 8] = d + rolled(d, 32)
    grads[ROWS_B1 + 8 :] = jnp.zeros((ROWS - ROWS_B1 - 8, 128), F32)


def unpack_kernel(grads, w1, b1, w2, b2):
    for t in range(27):
        block = grads[t * 16 : (t + 1) * 16]
        w2[t, 0:16] = block[:, :64]
        w2[t, 16:32] = rolled(block, 64)[:, :64]
    body = grads[ROWS_W1 : ROWS_W1 + 40]
    for ky in range(3):
        part = rolled(body, (128 - 32 * ky) % 128) if ky else body
        for kd in range(3):
            for kx in range(3):
                at = (kd * 3 + kx) * C_IN
                w1[(kd * 3 + ky) * 3 + kx] = part[at : at + C_IN, :C_MID]
    b2[...] = grads[ROWS_B2 : ROWS_B2 + 1, :C_OUT]
    b1[...] = grads[ROWS_B1 : ROWS_B1 + 1, :C_MID]


def call(kernel, outs, *args, scratch=()):
    return pl.pallas_call(
        kernel,
        out_shape=[jax.ShapeDtypeStruct(s, t) for s, t in outs],
        in_specs=[VMEM] * len(args),
        out_specs=[VMEM] * len(outs),
        scratch_shapes=[pltpu.VMEM(s, t) for s, t in scratch],
        compiler_params=PARAMS,
    )(*args)


def summed_over_devices(grads):
    near = ("y", "x", "core")
    count = lax.axis_size(near)
    pieces = lax.all_to_all(grads.reshape(count, ROWS // count, 128), near, 0, 0)
    mine = jnp.sum(pieces, axis=0)
    far = lax.axis_size("z")
    pieces = lax.all_to_all(jnp.broadcast_to(mine[None], (far,) + mine.shape), "z", 0, 0)
    mine = jnp.sum(pieces, axis=0)
    whole = lax.all_to_all(jnp.broadcast_to(mine[None], (count,) + mine.shape), near, 0, 0)
    return whole.reshape(ROWS, 128)


def local(volume, w_first, b_first, w_second, b_second, cotangent):
    vol = volume[0]
    cot = jnp.transpose(cotangent[0], (1, 2, 3, 0))
    w1 = jnp.transpose(w_first, (2, 3, 4, 1, 0)).reshape(27 * C_IN, C_MID).astype(F32)
    w2 = jnp.transpose(w_second, (2, 3, 4, 1, 0)).reshape(27, C_MID, C_OUT)
    up, down = call(pack_kernel, [((BLOCKS, 8, 128), BF16)] * 2, vol, cot)
    space = ("x", "core")
    count = lax.axis_size(space)
    before = lax.ppermute(up, space, [(i, i + 1) for i in range(count - 1)])
    behind = lax.ppermute(down, space, [(i + 1, i) for i in range(count - 1)])
    t1, t2, t2g = call(
        weights_kernel,
        [((256, 384), BF16), ((256, 1280), BF16), ((384, 768), BF16)],
        w1, b_first[None], w2, b_second[None],
    )
    feat, grads = call(
        main_kernel,
        [((2, 2, 32, C_OUT), BF16), ((ROWS, 128), F32)],
        vol, before, behind, cot, t1, t2, t2g,
        scratch=[
            ((384, 2048), BF16),
            ((256, 1024), F32),
            ((1280, 512), BF16),
            ((768, 512), BF16),
            ((256, 1024), BF16),
        ],
    )
    grads = summed_over_devices(grads)
    gw1, gb1, gw2, gb2 = call(
        unpack_kernel,
        [((27, C_IN, C_MID), F32), ((1, C_MID), F32), ((27, C_MID, C_OUT), F32), ((1, C_OUT), F32)],
        grads,
    )
    gw1 = jnp.transpose(gw1.reshape(3, 3, 3, C_IN, C_MID), (4, 3, 0, 1, 2))
    gw2 = jnp.transpose(gw2.reshape(3, 3, 3, C_MID, C_OUT), (4, 3, 0, 1, 2))
    return jnp.transpose(feat, (3, 0, 1, 2))[None], gw1, gb1[0], gw2, gb2[0]


def solution(mesh):
    dp, space = mesh.devices.shape
    y = 4 if dp % 4 == 0 else 1
    grid = Mesh(mesh.devices.reshape(dp // y, y, space // 2, 2), ("z", "y", "x", "core"))
    data = P(("z", "y"), None, ("x", "core"), None, None)
    return jax.shard_map(
        local,
        mesh=grid,
        in_specs=(data, P(), P(), P(), P(), data),
        out_specs=(data, P(), P(), P(), P()),
        check_vma=False,
    )
```

time: 559 us -> 75 us (0.13); the launches traced: 548 us -> 74.5 us
  waiting for transfers between devices: 278 us -> 0.01 us
  matrix products: 71.1 us -> 0 us
  blocking collectives: 109 us -> 55.2 us
  local copies, waits for them, and re-layouts: 44.9 us -> 2.51 us
  between operations: 14.8 us -> 0.74 us
  other arithmetic: 11 us -> 0.81 us
  starting transfers between devices: 19.7 us -> 10.2 us
    psum x1 -> x0, waiting for transfers between devices: 275 us -> none  [local(): lax.psum((grad_w_first, grad_b_first, grad_w_second, grad_b_second), ('dp...]
    psum x1 -> x0, blocking collectives: 109 us -> none  [local(): lax.psum((grad_w_first, grad_b_first, grad_w_second, grad_b_second), ('dp...]
    transpose x2 -> x0, matrix products: 57.6 us -> none  [weight_grad(): return jnp.transpose(result, (1, 0, 2, 3, 4))]
    all_to_all x0 -> x3, blocking collectives: none -> 55.2 us  [the longest x1 26.9 us: summed_over_devices(): lax.all_to_all(jnp.broadcast_to(mine[None], (far,) + mine.shape), 'z', 0, 0)]
    broadcast_in_dim x6 -> x2, local copies, waits for them, and re-layouts: 25.4 us -> 0.03 us  [the longest x1 0.02 us: summed_over_devices(): jnp.broadcast_to(mine[None], (count,) + mine.shape)]
    conv_general_dilated x3 -> x0, matrix products: 13.5 us -> none  [conv_valid(): lax.conv_general_dilated(padded[None], weights, (1, 1, 1), 'VALID', dimen...]
    ppermute x6 -> x2, starting transfers between devices: 19.7 us -> 10.2 us  [the longest x1 5.57 us: local(): behind = lax.ppermute(down, space, [(i + 1, i) for i in range(count - 1)])]
    reduce_sum x4 -> x2, other arithmetic: 7.04 us -> 0.05 us  [summed_over_devices(): mine = jnp.sum(pieces, axis=0)]
  transfers between devices with their start and end apart: 7 -> 2, of which waited for: 2 -> 0; matrix products, arithmetic and copies ran while one was open for 17% -> 1% of each run, Pallas kernels for 0% -> 1%
where the time goes in v1:
time: 75 us; the launch traced here: 74.5 us
  blocking collectives  55.2 us (74%)
  starting transfers between devices  10.2 us (14%)
  Pallas kernels  5.01 us (7%)
  local copies, waits for them, and re-layouts  2.51 us (3%)
  other arithmetic  0.81 us (1%)
    all_to_all x1, blocking collectives, summed_over_devices(): lax.all_to_all(jnp.broadcast_to(mine[None], (far,) + mine.shape), 'z', 0, 0)  26.9 us
    all_to_all x1, blocking collectives, summed_over_devices(): lax.all_to_all(jnp.broadcast_to(mine[None], (count,) + mine.shape), near,...  15.1 us
    all_to_all x1, blocking collectives, summed_over_devices(): lax.all_to_all(grads.reshape(count, ROWS // count, 128), near, 0, 0)  13.2 us
    ppermute x1, starting transfers between devices, local(): behind = lax.ppermute(down, space, [(i + 1, i) for i in range(count - 1)])  5.57 us
    pallas_call x4, Pallas kernels, call(): pl.pallas_call(kernel, out_shape=[jax.ShapeDtypeStruct(s, t) for s, t in...  5.01 us
    ppermute x1, starting transfers between devices, local(): before = lax.ppermute(up, space, [(i, i + 1) for i in range(count - 1)])  4.63 us
    unnamed x14, local copies, waits for them, and re-layouts  2.46 us
  transfers between devices with their start and end apart: 2, of which 0 were waited for; matrix products, arithmetic and copies ran while one was open for 1% of the time, Pallas kernels for 1%

profile of v1, /device:TPU:1, one launch (start us, length us, event | category | flops | bytes accessed | tf_op | source)
XLA Modules:
  0.0 74.5 jit_solution(12703310601012536398)
XLA Ops:
  0.6 0.0 copy-start
  0.6 0.8 %copy-done = bf16[1,4,8,8,128]{4,3,2,1,0:T(8,128)(2,1)S(1)} copy-done((bf16[1,4,8,8,128]{4,3,2,1,0:T(8,128)(2,1)S(1)}, bf16[1,4,8,8,128]{4,3,2,1,0:T(8,128)(2,1)}, u32[]{:S(2)}) %copy-start) | copy-done | bytes 65560
  1.5 0.0 copy-start.3
  1.5 0.8 %copy-done.3 = bf16[1,64,2,2,32]{1,4,3,2,0:T(8,128)(2,1)S(1)} copy-done((bf16[1,64,2,2,32]{1,4,3,2,0:T(8,128)(2,1)S(1)}, bf16[1,64,2,2,32]{1,4,3,2,0:T(8,128)(2,1)}, u32[]{:S(2)}) %copy-start.3) | copy-done | bytes 16408
  2.2 0.0 copy-start.2
  2.2 0.1 shard_map.101
  2.3 4.6 %collective-permute-start = (bf16[25,8,128]{2,1,0:T(8,128)(2,1)S(1)}, bf16[25,8,128]{2,1,0:T(8,128)(2,1)S(1)}, u32[]{:S(2)}, u32[]{:S(2)}) collective-permute-start(bf16[25,8,128]{2,1,0:T(8,128)(2,1)S(1)} %get-tuple-element.16), channel_id=1, source_target_pairs={{0,1},{1,2},{2,3},{3,4},{4,5},{5,6},{6,7},{8,9},{9,10},{10,11},{11... | collective-permute-start | bytes 153608 | tf_op jit(solution)/shard_map/ppermute | solution.py:282
  6.9 5.6 %collective-permute-start.1 = (bf16[25,8,128]{2,1,0:T(8,128)(2,1)S(1)}, bf16[25,8,128]{2,1,0:T(8,128)(2,1)S(1)}, u32[]{:S(2)}, u32[]{:S(2)}) collective-permute-start(bf16[25,8,128]{2,1,0:T(8,128)(2,1)S(1)} %get-tuple-element.17), channel_id=1, source_target_pairs={{1,0},{2,1},{3,2},{4,3},{5,4},{6,5},{7,6},{9,8},{10,9},{11,10},{12... | collective-permute-start | bytes 153608 | tf_op jit(solution)/shard_map/ppermute | solution.py:283
  12.5 0.8 %convert_bitcast_fusion = f32[3,3,3,4,32]{4,3,2,1,0:T(4,128)S(1)} fusion(bf16[32,4,3,3,3]{0,1,4,3,2:T(4,128)(2,1)} %param.7), kind=kLoop, calls=%fused_computation | loop fusion | flops 3456 | bytes 20736 | tf_op jit(solution)/shard_map/convert_element_type | solution.py:277
  13.3 0.0 copy-start.5
  13.3 0.0 copy-start.6
  13.3 0.0 copy-done.2
  13.3 0.6 copy-done.5
  14.0 0.0 copy-done.6
  14.0 0.0 copy-start.1
  14.0 0.0 copy-start.4
  14.0 0.6 shard_map.102
  14.6 0.0 collective-permute-done.before
  14.6 0.0 collective-permute-done.1.behind
  14.6 0.2 copy-done.1
  14.8 0.0 copy-done.4
  14.8 3.4 %shard_map.103 = (bf16[2,2,32,64]{3,2,1,0:T(8,128)(2,1)}, f32[512,128]{1,0:T(8,128)S(1)}) custom-call(bf16[4,8,8,128]{3,2,1,0:T(8,128)(2,1)S(1)} %bitcast.26, bf16[25,8,128]{2,1,0:T(8,128)(2,1)S(1)} %collective-permute-done.before, bf16[25,8,128]{2,1,0:T(8,128)(2,1)S(1)} %collective-permute-done.1.behind, bf16[2,2,32,64]{3,2,1,0:T(8,128)(2,1)S(1)} %bitcast.30, ...), custom_call_target="tpu_custom_call" | custom-call | tf_op jit(solution)/shard_map/pallas_call | solution.py:252
  18.3 13.2 %all_to_all.15 = f32[32,16,128]{2,1,0:T(8,128)S(1)} all-to-all(f32[32,16,128]{2,1,0:T(8,128)S(1)} %bitcast.27), channel_id=1, replica_groups=mesh['z'=16,'y'=4,'x'=4,'core'=2] {'y','x','core'}, dimensions={0} | all-to-all | bytes 524288 | tf_op jit(solution)/shard_map/all_to_all | solution.py:265
  31.5 26.9 %all_to_all.16 = f32[16,16,128]{2,1,0:T(8,128)S(1)} all-to-all(f32[16,16,128]{2,1,0:T(8,128)S(1)} %broadcast_in_dim.24), channel_id=1, replica_groups=mesh['z'=16,'y'=4,'x'=4,'core'=2] {'z'}, dimensions={0} | all-to-all | bytes 262144 | tf_op jit(solution)/shard_map/all_to_all | solution.py:268
  58.4 15.1 %all_to_all.17 = f32[32,16,128]{2,1,0:T(8,128)S(1)} all-to-all(f32[32,16,128]{2,1,0:T(8,128)S(1)} %broadcast_in_dim.25), channel_id=1, replica_groups=mesh['z'=16,'y'=4,'x'=4,'core'=2] {'y','x','core'}, dimensions={0} | all-to-all | bytes 524288 | tf_op jit(solution)/shard_map/all_to_all | solution.py:270
  73.6 0.9 %shard_map.104 = (f32[27,4,32]{2,1,0:T(4,128)}, f32[1,32]{1,0:T(1,128)}, f32[27,32,64]{2,1,0:T(8,128)}, f32[1,64]{1,0:T(1,128)}) custom-call(f32[512,128]{1,0:T(8,128)S(1)} %bitcast.24), custom_call_target="tpu_custom_call" | custom-call | tf_op jit(solution)/shard_map/pallas_call | solution.py:252
  (5 shorter events, 0.1 us)
Async XLA Ops:
  0.6 0.8 %copy-start = (bf16[1,4,8,8,128]{4,3,2,1,0:T(8,128)(2,1)S(1)}, bf16[1,4,8,8,128]{4,3,2,1,0:T(8,128)(2,1)}, u32[]{:S(2)}) copy-start(bf16[1,4,8,8,128]{4,3,2,1,0:T(8,128)(2,1)} %param.6) | copy-start | bytes 196612
  1.5 0.8 %copy-start.3 = (bf16[1,64,2,2,32]{1,4,3,2,0:T(8,128)(2,1)S(1)}, bf16[1,64,2,2,32]{1,4,3,2,0:T(8,128)(2,1)}, u32[]{:S(2)}) copy-start(bf16[1,64,2,2,32]{1,4,3,2,0:T(8,128)(2,1)} %param.11) | copy-start | bytes 49156
  2.2 11.1 %copy-start.2 = (bf16[64,32,3,3,3]{0,1,4,3,2:T(8,128)(2,1)S(1)}, bf16[64,32,3,3,3]{0,1,4,3,2:T(8,128)(2,1)}, u32[]{:S(2)}) copy-start(bf16[64,32,3,3,3]{0,1,4,3,2:T(8,128)(2,1)} %param.9) | copy-start | bytes 331780
  2.3 12.3 %collective-permute-start = (bf16[25,8,128]{2,1,0:T(8,128)(2,1)S(1)}, bf16[25,8,128]{2,1,0:T(8,128)(2,1)S(1)}, u32[]{:S(2)}, u32[]{:S(2)}) collective-permute-start(bf16[25,8,128]{2,1,0:T(8,128)(2,1)S(1)} %get-tuple-element.16), channel_id=1, source_target_pairs={{0,1},{1,2},{2,3},{3,4},{4,5},{5,6},{6,7},{8,9},{9,10},{10,11},{11... | collective-permute-start | bytes 153608 | tf_op jit(solution)/shard_map/ppermute | solution.py:282
  6.9 7.7 %collective-permute-start.1 = (bf16[25,8,128]{2,1,0:T(8,128)(2,1)S(1)}, bf16[25,8,128]{2,1,0:T(8,128)(2,1)S(1)}, u32[]{:S(2)}, u32[]{:S(2)}) collective-permute-start(bf16[25,8,128]{2,1,0:T(8,128)(2,1)S(1)} %get-tuple-element.17), channel_id=1, source_target_pairs={{1,0},{2,1},{3,2},{4,3},{5,4},{6,5},{7,6},{9,8},{10,9},{11,10},{12... | collective-permute-start | bytes 153608 | tf_op jit(solution)/shard_map/ppermute | solution.py:283
  13.3 0.7 copy-start.5
  13.3 0.7 copy-start.6
  14.0 0.8 %copy-start.1 = (bf16[1,4,8,8,128]{4,3,2,1,0:T(8,128)(2,1)S(1)}, bf16[1,4,8,8,128]{4,3,2,1,0:T(8,128)(2,1)}, u32[]{:S(2)}) copy-start(bf16[1,4,8,8,128]{4,3,2,1,0:T(8,128)(2,1)} %param.6) | copy-start | bytes 196612
  14.0 0.8 %copy-start.4 = (bf16[1,64,2,2,32]{1,4,3,2,0:T(8,128)(2,1)S(1)}, bf16[1,64,2,2,32]{1,4,3,2,0:T(8,128)(2,1)}, u32[]{:S(2)}) copy-start(bf16[1,64,2,2,32]{1,4,3,2,0:T(8,128)(2,1)} %param.11) | copy-start | bytes 49156

commit v2 on v1

--- a/solution.py
+++ b/solution.py
@@ -24,17 +24,16 @@
     return lax.broadcasted_iota(jnp.int32, shape, dim)
 
 
-def split(v):
-    hi = v.astype(BF16)
-    return hi, (v - hi.astype(F32)).astype(BF16)
-
-
 def leaky(v):
     return jnp.where(v > 0.0, v, 0.3 * v)
 
 
 def rolled(v, shift):
     return pltpu.roll(v, shift, 1)
+
+
+def paired(v):
+    return ((v + rolled(v, v.shape[1] - 1)) * 0.125).astype(BF16)
 
 
 def taps(v, period):
@@ -44,14 +43,29 @@
     return before, v, after
 
 
-def pack_kernel(vol, cot, up, down):
-    for c in range(C_IN):
-        up[c * DEEP : (c + 1) * DEEP] = vol[c, 8 - DEEP :]
-        down[c * DEEP : (c + 1) * DEEP] = vol[c, :DEEP]
-    for ref, d in ((up, 1), (down, 0)):
-        both = jnp.concatenate([cot[d, 0].astype(F32), cot[d, 1].astype(F32)], axis=1)
-        ref[COT_AT:ONES_AT] = both.reshape(4, 8, 128).astype(BF16)
-        ref[ONES_AT] = jnp.ones((8, 128), BF16)
+def pack_kernel(vol_at, cot_at, w1_at, b1_at, w2_at, b2_at, across, inside, vol, cot, w1, b1, w2, b2, sems):
+    pairs = ((vol_at, vol), (cot_at, cot), (w1_at, w1), (b1_at, b1), (w2_at, w2), (b2_at, b2))
+    copies = [pltpu.make_async_copy(a, b, sems.at[i]) for i, (a, b) in enumerate(pairs)]
+    for copy in copies:
+        copy.start()
+    across[ONES_AT] = jnp.ones((8, 128), BF16)
+    inside[ONES_AT] = jnp.ones((8, 128), BF16)
+    copies[0].wait()
+    copies[1].wait()
+
+    def fill(first, last):
+        for c in range(C_IN):
+            first[c * DEEP : (c + 1) * DEEP] = vol[c, :DEEP]
+            last[c * DEEP : (c + 1) * DEEP] = vol[c, 8 - DEEP :]
+        for ref, d in ((first, 0), (last, 1)):
+            both = jnp.concatenate([cot[d, 0].astype(F32), cot[d, 1].astype(F32)], axis=1)
+            ref[COT_AT:ONES_AT] = both.reshape(4, 8, 128).astype(BF16)
+
+    core = lax.axis_index("core")
+    pl.when(core == 0)(lambda: fill(across, inside))
+    pl.when(core == 1)(lambda: fill(inside, across))
+    for copy in copies[2:]:
+        copy.wait()
 
 
 def bias_rows(bias, copies):
@@ -65,7 +79,8 @@
 
 
 def weights_kernel(w1, b1, w2, b2, t1, t2, t2g):
-    wide = jnp.concatenate([w1[...]] * 4, axis=1)
+    narrow = jnp.concatenate([w1[t].astype(F32) for t in range(27)], axis=0)
+    wide = jnp.concatenate([narrow] * 4, axis=1)
     y_in = iota((8, 128), 0)
     lanes = iota((8, 128), 1) // C_MID
     blocks = []
@@ -81,7 +96,7 @@
                         total = jnp.where(ky == k, wide[at : at + 1], total)
                     halves.append(total)
                 blocks.append(jnp.concatenate(halves, axis=1))
-    body = jnp.concatenate(blocks + [bias_rows(b1[...], 8)[:96]], axis=0)
+    body = jnp.concatenate(blocks + [bias_rows(b1[...].reshape(1, C_MID), 8)[:96]], axis=0)
     t1[...] = body.T.astype(BF16)
     nothing = jnp.zeros((C_MID, C_OUT), F32)
     for kd in range(3):
@@ -102,10 +117,17 @@
             t2g[kd * 128 : (kd + 1) * 128, kx * 256 : (kx + 1) * 256] = block.astype(BF16)
             at = (kd * 3 + kx) * 128
             t2[:, at : at + 128] = block.T.astype(BF16)
-    t2[:, 1152:] = bias_rows(b2[...], 4).T.astype(BF16)
-
-
-def main_kernel(vol, before, behind, cot, t1, t2, t2g, feat, grads, p1, pre1, p2, g4x, g1):
+    t2[:, 1152:] = bias_rows(b2[...].reshape(1, C_OUT), 4).T.astype(BF16)
+
+
+def main_kernel(vol, across, inside, cot, t1, t2, t2g, feat, grads, before, behind, p1, pre1, p2, g4x, g1):
+    def place(first, second):
+        before[...] = first[...]
+        behind[...] = second[...]
+
+    core = lax.axis_index("core")
+    pl.when(core == 0)(lambda: place(across, inside))
+    pl.when(core == 1)(lambda: place(inside, across))
     lane = iota((1, 128), 1)
     low = lane < 64
 
@@ -124,29 +146,25 @@
                 p1[kd * 96 : (kd + 1) * 96, to * 128 : (to + 1) * 128] = stack
     p1[288:, :] = jnp.ones((96, 2048), BF16)
 
-    his, los = [], []
+    pooled = []
     for d in range(8):
         pre = dot(t1[...], p1[:, d * 256 : (d + 1) * 256])
         if 2 <= d < 6:
             pre1[:, (d - 2) * 256 : (d - 1) * 256] = pre
         act = leaky(pre).reshape(4, 2, C_MID, 256)
         act = (act[:, 0] + act[:, 1]).reshape(128, 256)
-        hi, lo = split(act[:, :128] + act[:, 128:])
-        his.append(hi)
-        los.append(lo)
+        pooled.append(paired(act[:, :128] + act[:, 128:]))
 
     row, col = iota((256, 128), 0), iota((256, 128), 1)
-    pool = jnp.where((row // 128 == col // 64) & (row % 128 // 2 == col % 64), 0.125, 0.0).astype(BF16)
+    pool = jnp.where((row // 128 == col // 64) & (row % 128 == col % 64 * 2), 1.0, 0.0).astype(BF16)
     m_before = before[ONES_AT].astype(F32)[:1]
     m_behind = behind[ONES_AT].astype(F32)[:1]
     for r in range(6):
-        act = dot(jnp.concatenate([his[r], his[r + 2]], axis=1), pool)
-        act = act + dot(jnp.concatenate([los[r], los[r + 2]], axis=1), pool)
+        act = dot(jnp.concatenate([pooled[r], pooled[r + 2]], axis=1), pool)
         if r < 2:
             act = act * jnp.where(low, m_before, 1.0)
         if r >= 4:
             act = act * jnp.where(low, 1.0, m_behind)
-        act = act.astype(BF16).astype(F32)
         stack = jnp.concatenate(taps(act, 64), axis=0).astype(BF16)
         for kd in range(3):
             to = r - kd
@@ -160,10 +178,9 @@
     act = act[:, 0] + act[:, 1]
     act = act[:, :, :128] + act[:, :, 128:]
     row, col = iota((64, 128), 0), iota((64, 128), 1)
-    pool = jnp.where((row // 32 == col // 64) & (row % 32 == col % 64 // 2), 0.125, 0.0).astype(BF16)
+    pool = jnp.where((row // 32 == col // 64) & (row % 32 * 2 == col % 64), 1.0, 0.0).astype(BF16)
     for y in range(2):
-        hi, lo = split(act[y])
-        out = dot(pool, hi, ((1,), (1,))) + dot(pool, lo, ((1,), (1,)))
+        out = dot(pool, paired(act[y]), ((1,), (1,)))
         for d in range(2):
             feat[d, y] = out[d * 32 : (d + 1) * 32].astype(BF16)
 
@@ -248,13 +265,13 @@
     b1[...] = grads[ROWS_B1 : ROWS_B1 + 1, :C_MID]
 
 
-def call(kernel, outs, *args, scratch=()):
+def call(kernel, outs, *args, scratch=(), place=pltpu.VMEM):
     return pl.pallas_call(
         kernel,
         out_shape=[jax.ShapeDtypeStruct(s, t) for s, t in outs],
-        in_specs=[VMEM] * len(args),
+        in_specs=[pl.BlockSpec(memory_space=place)] * len(args),
         out_specs=[VMEM] * len(outs),
-        scratch_shapes=[pltpu.VMEM(s, t) for s, t in scratch],
+        scratch_shapes=scratch,
         compiler_params=PARAMS,
     )(*args)
 
@@ -272,30 +289,40 @@
 
 
 def local(volume, w_first, b_first, w_second, b_second, cotangent):
-    vol = volume[0]
     cot = jnp.transpose(cotangent[0], (1, 2, 3, 0))
-    w1 = jnp.transpose(w_first, (2, 3, 4, 1, 0)).reshape(27 * C_IN, C_MID).astype(F32)
+    w1 = jnp.transpose(w_first, (2, 3, 4, 1, 0)).reshape(27, C_IN, C_MID)
     w2 = jnp.transpose(w_second, (2, 3, 4, 1, 0)).reshape(27, C_MID, C_OUT)
-    up, down = call(pack_kernel, [((BLOCKS, 8, 128), BF16)] * 2, vol, cot)
+    args = [pltpu.with_memory_space_constraint(a, pltpu.HBM) for a in (volume[0], cot, w1, b_first, w2, b_second)]
+    across, inside, vol, cot, w1, b1, w2, b2 = call(
+        pack_kernel,
+        [((BLOCKS, 8, 128), BF16)] * 2 + [(a.shape, a.dtype) for a in args],
+        *args,
+        scratch=[pltpu.SemaphoreType.DMA((len(args),))],
+        place=pltpu.HBM,
+    )
     space = ("x", "core")
     count = lax.axis_size(space)
-    before = lax.ppermute(up, space, [(i, i + 1) for i in range(count - 1)])
-    behind = lax.ppermute(down, space, [(i + 1, i) for i in range(count - 1)])
+    pairs = [(i, i + 1) for i in range(1, count - 1, 2)]
+    across = lax.ppermute(across, space, pairs + [(j, i) for i, j in pairs])
+    pairs = [(i, i + 1) for i in range(0, count, 2)]
+    inside = lax.ppermute(inside, space, pairs + [(j, i) for i, j in pairs])
     t1, t2, t2g = call(
         weights_kernel,
         [((256, 384), BF16), ((256, 1280), BF16), ((384, 768), BF16)],
-        w1, b_first[None], w2, b_second[None],
+        w1, b1, w2, b2,
     )
     feat, grads = call(
         main_kernel,
         [((2, 2, 32, C_OUT), BF16), ((ROWS, 128), F32)],
-        vol, before, behind, cot, t1, t2, t2g,
+        vol, across, inside, cot, t1, t2, t2g,
         scratch=[
-            ((384, 2048), BF16),
-            ((256, 1024), F32),
-            ((1280, 512), BF16),
-            ((768, 512), BF16),
-            ((256, 1024), BF16),
+            pltpu.VMEM((BLOCKS, 8, 128), BF16),
+            pltpu.VMEM((BLOCKS, 8, 128), BF16),
+            pltpu.VMEM((384, 2048), BF16),
+            pltpu.VMEM((256, 1024), F32),
+            pltpu.VMEM((1280, 512), BF16),
+            pltpu.VMEM((768, 512), BF16),
+            pltpu.VMEM((256, 1024), BF16),
         ],
     )
     grads = summed_over_devices(grads)

time: 75 us -> 71.8 us (0.957)
  local copies, waits for them, and re-layouts: 2.51 us -> 0.03 us
  Pallas kernels: 5.01 us -> 6.04 us
  other arithmetic: 0.81 us -> 0.05 us
  starting transfers between devices: 10.2 us -> 9.45 us
    unnamed x14 -> x0, local copies, waits for them, and re-layouts: 2.46 us -> none
    pallas_call x4, Pallas kernels: 5.01 us -> 6.04 us  [call(): pl.pallas_call(kernel, out_shape=[jax.ShapeDtypeStruct(s, t) for s, t in...]
    convert_element_type x1 -> x0, other arithmetic: 0.75 us -> none  [local(): jnp.transpose(w_first, (2, 3, 4, 1, 0)).reshape(27 * C_IN, C_MID)]
  transfers between devices with their start and end apart: 2 -> 2, of which waited for: 0 -> 1; matrix products, arithmetic and copies ran while one was open for 1% -> 0% of each run, Pallas kernels for 1% -> 1%
where the time goes in v2:
time: 71.8 us; the launch traced here: 71.5 us
  blocking collectives  55 us (77%)
  starting transfers between devices  9.45 us (13%)
  Pallas kernels  6.04 us (8%)
    all_to_all x1, blocking collectives, summed_over_devices(): lax.all_to_all(jnp.broadcast_to(mine[None], (far,) + mine.shape), 'z', 0, 0)  26.9 us
    all_to_all x1, blocking collectives, summed_over_devices(): lax.all_to_all(jnp.broadcast_to(mine[None], (count,) + mine.shape), near,...  15.1 us
    all_to_all x1, blocking collectives, summed_over_devices(): lax.all_to_all(grads.reshape(count, ROWS // count, 128), near, 0, 0)  13 us
    pallas_call x4, Pallas kernels, call(): pl.pallas_call(kernel, out_shape=[jax.ShapeDtypeStruct(s, t) for s, t in...  6.04 us
    ppermute x1, starting transfers between devices, local(): inside = lax.ppermute(inside, space, pairs + [(j, i) for i, j in pairs])  4.94 us
    ppermute x1, starting transfers between devices, local(): across = lax.ppermute(across, space, pairs + [(j, i) for i, j in pairs])  4.51 us
  transfers between devices with their start and end apart: 2, of which 1 were waited for; matrix products, arithmetic and copies ran while one was open for 0% of the time, Pallas kernels for 1%

profile of v2, /device:TPU:1, one launch (start us, length us, event | category | flops | bytes accessed | tf_op | source)
XLA Modules:
  0.0 71.5 jit_solution(5446809801982841597)
XLA Ops:
  0.6 1.1 %shard_map.101 = (bf16[25,8,128]{2,1,0:T(8,128)(2,1)S(1)}, bf16[25,8,128]{2,1,0:T(8,128)(2,1)S(1)}, bf16[4,8,8,128]{3,2,1,0:T(8,128)(2,1)S(1)}, bf16[2,2,32,64]{...) custom-call(bf16[4,8,8,128]{3,2,1,0:T(8,128)(2,1)} %bitcast.26, ...), custom_call_target="tpu_custom_call" | custom-call | tf_op jit(solution)/shard_map/pallas_call | solution.py:269
  1.7 4.5 %collective-permute-start = (bf16[25,8,128]{2,1,0:T(8,128)(2,1)S(1)}, bf16[25,8,128]{2,1,0:T(8,128)(2,1)S(1)}, u32[]{:S(2)}, u32[]{:S(2)}) collective-permute-start(bf16[25,8,128]{2,1,0:T(8,128)(2,1)S(1)} %get-tuple-element.23), channel_id=1, source_target_pairs={{1,2},{3,4},{5,6},{2,1},{4,3},{6,5},{9,10},{11,12},{13,14},{10,9},... | collective-permute-start | bytes 153608 | tf_op jit(solution)/shard_map/ppermute | solution.py:306
  6.2 4.9 %collective-permute-start.1 = (bf16[25,8,128]{2,1,0:T(8,128)(2,1)S(1)}, bf16[25,8,128]{2,1,0:T(8,128)(2,1)S(1)}, u32[]{:S(2)}, u32[]{:S(2)}) collective-permute-start(bf16[25,8,128]{2,1,0:T(8,128)(2,1)S(1)} %get-tuple-element.24), channel_id=1, source_target_pairs={{0,1},{2,3},{4,5},{6,7},{1,0},{3,2},{5,4},{7,6},{8,9},{10,11},{12,... | collective-permute-start | bytes 153608 | tf_op jit(solution)/shard_map/ppermute | solution.py:308
  11.2 0.6 shard_map.102
  11.8 0.0 collective-permute-done.across
  11.8 0.3 collective-permute-done.1.inside
  12.1 3.5 %shard_map.103 = (bf16[2,2,32,64]{3,2,1,0:T(8,128)(2,1)}, f32[512,128]{1,0:T(8,128)S(1)}) custom-call(bf16[4,8,8,128]{3,2,1,0:T(8,128)(2,1)S(1)} %get-tuple-element.22.vol, bf16[25,8,128]{2,1,0:T(8,128)(2,1)S(1)} %collective-permute-done.across, bf16[25,8,128]{2,1,0:T(8,128)(2,1)S(1)} %collective-permute-done.1.inside, ...), custom_call_target="tpu_custom_call" | custom-call | tf_op jit(solution)/shard_map/pallas_call | solution.py:269
  15.5 13.0 %all_to_all.15 = f32[32,16,128]{2,1,0:T(8,128)S(1)} all-to-all(f32[32,16,128]{2,1,0:T(8,128)S(1)} %bitcast.24), channel_id=1, replica_groups=mesh['z'=16,'y'=4,'x'=4,'core'=2] {'y','x','core'}, dimensions={0} | all-to-all | bytes 524288 | tf_op jit(solution)/shard_map/all_to_all | solution.py:282
  28.5 26.9 %all_to_all.16 = f32[16,16,128]{2,1,0:T(8,128)S(1)} all-to-all(f32[16,16,128]{2,1,0:T(8,128)S(1)} %broadcast_in_dim.7), channel_id=1, replica_groups=mesh['z'=16,'y'=4,'x'=4,'core'=2] {'z'}, dimensions={0} | all-to-all | bytes 262144 | tf_op jit(solution)/shard_map/all_to_all | solution.py:285
  55.5 15.1 %all_to_all.17 = f32[32,16,128]{2,1,0:T(8,128)S(1)} all-to-all(f32[32,16,128]{2,1,0:T(8,128)S(1)} %broadcast_in_dim.8), channel_id=1, replica_groups=mesh['z'=16,'y'=4,'x'=4,'core'=2] {'y','x','core'}, dimensions={0} | all-to-all | bytes 524288 | tf_op jit(solution)/shard_map/all_to_all | solution.py:287
  70.6 0.9 %shard_map.104 = (f32[27,4,32]{2,1,0:T(4,128)}, f32[1,32]{1,0:T(1,128)}, f32[27,32,64]{2,1,0:T(8,128)}, f32[1,64]{1,0:T(1,128)}) custom-call(f32[512,128]{1,0:T(8,128)S(1)} %bitcast.23), custom_call_target="tpu_custom_call" | custom-call | tf_op jit(solution)/shard_map/pallas_call | solution.py:269
  (4 shorter events, 0.1 us)
Async XLA Ops:
  1.7 10.1 %collective-permute-start = (bf16[25,8,128]{2,1,0:T(8,128)(2,1)S(1)}, bf16[25,8,128]{2,1,0:T(8,128)(2,1)S(1)}, u32[]{:S(2)}, u32[]{:S(2)}) collective-permute-start(bf16[25,8,128]{2,1,0:T(8,128)(2,1)S(1)} %get-tuple-element.23), channel_id=1, source_target_pairs={{1,2},{3,4},{5,6},{2,1},{4,3},{6,5},{9,10},{11,12},{13,14},{10,9},... | collective-permute-start | bytes 153608 | tf_op jit(solution)/shard_map/ppermute | solution.py:306
  6.2 5.8 %collective-permute-start.1 = (bf16[25,8,128]{2,1,0:T(8,128)(2,1)S(1)}, bf16[25,8,128]{2,1,0:T(8,128)(2,1)S(1)}, u32[]{:S(2)}, u32[]{:S(2)}) collective-permute-start(bf16[25,8,128]{2,1,0:T(8,128)(2,1)S(1)} %get-tuple-element.24), channel_id=1, source_target_pairs={{0,1},{2,3},{4,5},{6,7},{1,0},{3,2},{5,4},{7,6},{8,9},{10,11},{12,... | collective-permute-start | bytes 153608 | tf_op jit(solution)/shard_map/ppermute | solution.py:308

commit v3 on v2

--- a/solution.py
+++ b/solution.py
@@ -13,7 +13,7 @@
 COT_AT = C_IN * DEEP
 ONES_AT = COT_AT + 4
 BLOCKS = ONES_AT + 1
-ROWS_W2, ROWS_W1, ROWS_B2, ROWS_B1, ROWS = 0, 432, 472, 480, 512
+ROWS_W2, ROWS_W1, ROWS_B, ROWS = 0, 432, 480, 512
 
 
 def dot(a, b, dims=((1,), (0,))):
@@ -25,7 +25,7 @@
 
 
 def leaky(v):
-    return jnp.where(v > 0.0, v, 0.3 * v)
+    return jnp.maximum(v, 0.3 * v)
 
 
 def rolled(v, shift):
@@ -228,9 +228,9 @@
                 odd = [block(y, p) for p in range(2) for y in [2 * p + ky] if 0 <= y < 4]
                 total = sum(even[1:], even[0]) + rolled(sum(odd[1:], odd[0]), 64)
                 at = ROWS_W2 + ((kd * 3 + ky) * 3 + kx) * 16
-                grads[at : at + 16] = jnp.where(low, total[:16], rolled(total[16:], 64))
-    d = d2[1152:1160, :128] + d2[1152:1160, 128:]
-    grads[ROWS_B2 : ROWS_B2 + 8] = d + rolled(d, 64)
+                grads[at : at + 16] = jnp.where(low, total[:16], rolled(total[16:], 64)).astype(BF16)
+    bias2 = d2[1152:1160, :128] + d2[1152:1160, 128:]
+    bias2 = bias2 + rolled(bias2, 64)
 
     d1 = dot(p1[0:304, 512:1536], g1[...], ((1,), (1,)))
     body = d1[:288].reshape(36, 8, 256)
@@ -242,27 +242,30 @@
         part = part + rolled(part, 64)
         part = part + rolled(part, 32)
         total = jnp.where(lane // 32 == k, part, total)
-    grads[ROWS_W1 : ROWS_W1 + 40] = jnp.concatenate([total, jnp.zeros((4, 128), F32)], axis=0)
-    d = d1[288:296, :128] + d1[288:296, 128:]
-    d = d + rolled(d, 64)
-    grads[ROWS_B1 : ROWS_B1 + 8] = d + rolled(d, 32)
-    grads[ROWS_B1 + 8 :] = jnp.zeros((ROWS - ROWS_B1 - 8, 128), F32)
+    total = jnp.concatenate([total, jnp.zeros((12, 128), F32)], axis=0)
+    grads[ROWS_W1 : ROWS_W1 + 48] = total.astype(BF16)
+    bias1 = d1[288:296, :128] + d1[288:296, 128:]
+    bias1 = bias1 + rolled(bias1, 64)
+    bias1 = bias1 + rolled(bias1, 32)
+    grads[ROWS_B : ROWS_B + 16] = jnp.concatenate([bias2, bias1], axis=0).astype(BF16)
+    grads[ROWS_B + 16 :] = jnp.zeros((ROWS - ROWS_B - 16, 128), BF16)
 
 
 def unpack_kernel(grads, w1, b1, w2, b2):
     for t in range(27):
-        block = grads[t * 16 : (t + 1) * 16]
+        block = grads[t * 16 : (t + 1) * 16].astype(F32)
         w2[t, 0:16] = block[:, :64]
         w2[t, 16:32] = rolled(block, 64)[:, :64]
-    body = grads[ROWS_W1 : ROWS_W1 + 40]
+    body = grads[ROWS_W1 : ROWS_W1 + 48].astype(F32)
     for ky in range(3):
         part = rolled(body, (128 - 32 * ky) % 128) if ky else body
         for kd in range(3):
             for kx in range(3):
                 at = (kd * 3 + kx) * C_IN
                 w1[(kd * 3 + ky) * 3 + kx] = part[at : at + C_IN, :C_MID]
-    b2[...] = grads[ROWS_B2 : ROWS_B2 + 1, :C_OUT]
-    b1[...] = grads[ROWS_B1 : ROWS_B1 + 1, :C_MID]
+    body = grads[ROWS_B : ROWS_B + 16].astype(F32)
+    b2[...] = body[:1, :C_OUT]
+    b1[...] = body[8:9, :C_MID]
 
 
 def call(kernel, outs, *args, scratch=(), place=pltpu.VMEM):
@@ -276,16 +279,24 @@
     )(*args)
 
 
+def sum_kernel(pieces, out):
+    total = pieces[0].astype(F32)
+    for i in range(1, pieces.shape[0]):
+        total = total + pieces[i].astype(F32)
+    total = total.astype(BF16)
+    for i in range(out.shape[0]):
+        out[i] = total
+
+
 def summed_over_devices(grads):
     near = ("y", "x", "core")
-    count = lax.axis_size(near)
-    pieces = lax.all_to_all(grads.reshape(count, ROWS // count, 128), near, 0, 0)
-    mine = jnp.sum(pieces, axis=0)
-    far = lax.axis_size("z")
-    pieces = lax.all_to_all(jnp.broadcast_to(mine[None], (far,) + mine.shape), "z", 0, 0)
-    mine = jnp.sum(pieces, axis=0)
-    whole = lax.all_to_all(jnp.broadcast_to(mine[None], (count,) + mine.shape), near, 0, 0)
-    return whole.reshape(ROWS, 128)
+    count, far = lax.axis_size(near), lax.axis_size("z")
+    rows = ROWS // count
+    pieces = lax.all_to_all(grads.reshape(count, rows, 128), near, 0, 0)
+    (mine,) = call(sum_kernel, [((far, rows, 128), BF16)], pieces)
+    pieces = lax.all_to_all(mine, "z", 0, 0)
+    (mine,) = call(sum_kernel, [((count, rows, 128), BF16)], pieces)
+    return lax.all_to_all(mine, near, 0, 0).reshape(ROWS, 128)
 
 
 def local(volume, w_first, b_first, w_second, b_second, cotangent):
@@ -313,7 +324,7 @@
     )
     feat, grads = call(
         main_kernel,
-        [((2, 2, 32, C_OUT), BF16), ((ROWS, 128), F32)],
+        [((2, 2, 32, C_OUT), BF16), ((ROWS, 128), BF16)],
         vol, across, inside, cot, t1, t2, t2g,
         scratch=[
             pltpu.VMEM((BLOCKS, 8, 128), BF16),

time: 71.8 us -> 67.6 us (0.942)
  blocking collectives: 55 us -> 50.8 us
    all_to_all x3, blocking collectives: 55 us -> 50.8 us  [the longest x1 26.3 us: summed_over_devices(): pieces = lax.all_to_all(mine, 'z', 0, 0)]
    pallas_call x4 -> x6, Pallas kernels: 6.04 us -> 6.08 us  [call(): pl.pallas_call(kernel, out_shape=[jax.ShapeDtypeStruct(s, t) for s, t in...]
where the time goes in v3:
time: 67.6 us; the launch traced here: 67.3 us
  blocking collectives  50.8 us (75%)
  starting transfers between devices  9.45 us (14%)
  Pallas kernels  6.08 us (9%)
  between operations  0.68 us (1%)
    all_to_all x1, blocking collectives, summed_over_devices(): pieces = lax.all_to_all(mine, 'z', 0, 0)  26.3 us
    all_to_all x1, blocking collectives, summed_over_devices(): return lax.all_to_all(mine, near, 0, 0).reshape(ROWS, 128)  12.8 us
    all_to_all x1, blocking collectives, summed_over_devices(): pieces = lax.all_to_all(grads.reshape(count, rows, 128), near, 0, 0)  11.7 us
    pallas_call x6, Pallas kernels, call(): pl.pallas_call(kernel, out_shape=[jax.ShapeDtypeStruct(s, t) for s, t in...  6.08 us
    ppermute x1, starting transfers between devices, local(): inside = lax.ppermute(inside, space, pairs + [(j, i) for i, j in pairs])  4.94 us
    ppermute x1, starting transfers between devices, local(): across = lax.ppermute(across, space, pairs + [(j, i) for i, j in pairs])  4.51 us
  transfers between devices with their start and end apart: 2, of which 1 were waited for; matrix products, arithmetic and copies ran while one was open for 0% of the time, Pallas kernels for 1%

profile of v3, /device:TPU:1, one launch (start us, length us, event | category | flops | bytes accessed | tf_op | source)
XLA Modules:
  0.0 67.3 jit_solution(18008574758261262594)
XLA Ops:
  0.6 1.1 %shard_map.101 = (bf16[25,8,128]{2,1,0:T(8,128)(2,1)S(1)}, bf16[25,8,128]{2,1,0:T(8,128)(2,1)S(1)}, bf16[4,8,8,128]{3,2,1,0:T(8,128)(2,1)S(1)}, bf16[2,2,32,64]{...) custom-call(bf16[4,8,8,128]{3,2,1,0:T(8,128)(2,1)} %bitcast.26, ...), custom_call_target="tpu_custom_call" | custom-call | tf_op jit(solution)/shard_map/pallas_call | solution.py:272
  1.7 4.5 %collective-permute-start = (bf16[25,8,128]{2,1,0:T(8,128)(2,1)S(1)}, bf16[25,8,128]{2,1,0:T(8,128)(2,1)S(1)}, u32[]{:S(2)}, u32[]{:S(2)}) collective-permute-start(bf16[25,8,128]{2,1,0:T(8,128)(2,1)S(1)} %get-tuple-element.23), channel_id=1, source_target_pairs={{1,2},{3,4},{5,6},{2,1},{4,3},{6,5},{9,10},{11,12},{13,14},{10,9},... | collective-permute-start | bytes 153608 | tf_op jit(solution)/shard_map/ppermute | solution.py:317
  6.2 4.9 %collective-permute-start.1 = (bf16[25,8,128]{2,1,0:T(8,128)(2,1)S(1)}, bf16[25,8,128]{2,1,0:T(8,128)(2,1)S(1)}, u32[]{:S(2)}, u32[]{:S(2)}) collective-permute-start(bf16[25,8,128]{2,1,0:T(8,128)(2,1)S(1)} %get-tuple-element.24), channel_id=1, source_target_pairs={{0,1},{2,3},{4,5},{6,7},{1,0},{3,2},{5,4},{7,6},{8,9},{10,11},{12,... | collective-permute-start | bytes 153608 | tf_op jit(solution)/shard_map/ppermute | solution.py:319
  11.2 0.6 shard_map.102
  11.8 0.0 collective-permute-done.across
  11.8 0.3 collective-permute-done.1.inside
  12.1 3.5 %shard_map.103 = (bf16[2,2,32,64]{3,2,1,0:T(8,128)(2,1)}, bf16[512,128]{1,0:T(8,128)(2,1)S(1)}) custom-call(bf16[4,8,8,128]{3,2,1,0:T(8,128)(2,1)S(1)} %get-tuple-element.22.vol, bf16[25,8,128]{2,1,0:T(8,128)(2,1)S(1)} %collective-permute-done.across, bf16[25,8,128]{2,1,0:T(8,128)(2,1)S(1)} %collective-permute-done.1.inside, ...), custom_call_target="tpu_custom_call" | custom-call | tf_op jit(solution)/shard_map/pallas_call | solution.py:272
  15.5 11.7 %all_to_all.15.pieces = bf16[32,16,128]{2,1,0:T(8,128)(2,1)S(1)} all-to-all(bf16[32,16,128]{2,1,0:T(8,128)(2,1)S(1)} %bitcast.24), channel_id=1, replica_groups=mesh['z'=16,'y'=4,'x'=4,'core'=2] {'y','x','core'}, dimensions={0} | all-to-all | bytes 262144 | tf_op jit(solution)/shard_map/all_to_all | solution.py:295
  27.3 26.3 %all_to_all.16.pieces = bf16[16,16,128]{2,1,0:T(8,128)(2,1)S(1)} all-to-all(bf16[16,16,128]{2,1,0:T(8,128)(2,1)S(1)} %shard_map.104), channel_id=1, replica_groups=mesh['z'=16,'y'=4,'x'=4,'core'=2] {'z'}, dimensions={0} | all-to-all | bytes 131072 | tf_op jit(solution)/shard_map/all_to_all | solution.py:297
  53.6 12.8 %all_to_all.17 = bf16[32,16,128]{2,1,0:T(8,128)(2,1)S(1)} all-to-all(bf16[32,16,128]{2,1,0:T(8,128)(2,1)S(1)} %shard_map.105), channel_id=1, replica_groups=mesh['z'=16,'y'=4,'x'=4,'core'=2] {'y','x','core'}, dimensions={0} | all-to-all | bytes 262144 | tf_op jit(solution)/shard_map/all_to_all | solution.py:299
  66.4 0.9 %shard_map.106 = (f32[27,4,32]{2,1,0:T(4,128)}, f32[1,32]{1,0:T(1,128)}, f32[27,32,64]{2,1,0:T(8,128)}, f32[1,64]{1,0:T(1,128)}) custom-call(bf16[512,128]{1,0:T(8,128)(2,1)S(1)} %bitcast.23), custom_call_target="tpu_custom_call" | custom-call | tf_op jit(solution)/shard_map/pallas_call | solution.py:272
  (2 shorter events, 0.1 us)
Async XLA Ops:
  1.7 10.1 %collective-permute-start = (bf16[25,8,128]{2,1,0:T(8,128)(2,1)S(1)}, bf16[25,8,128]{2,1,0:T(8,128)(2,1)S(1)}, u32[]{:S(2)}, u32[]{:S(2)}) collective-permute-start(bf16[25,8,128]{2,1,0:T(8,128)(2,1)S(1)} %get-tuple-element.23), channel_id=1, source_target_pairs={{1,2},{3,4},{5,6},{2,1},{4,3},{6,5},{9,10},{11,12},{13,14},{10,9},... | collective-permute-start | bytes 153608 | tf_op jit(solution)/shard_map/ppermute | solution.py:317
  6.2 5.8 %collective-permute-start.1 = (bf16[25,8,128]{2,1,0:T(8,128)(2,1)S(1)}, bf16[25,8,128]{2,1,0:T(8,128)(2,1)S(1)}, u32[]{:S(2)}, u32[]{:S(2)}) collective-permute-start(bf16[25,8,128]{2,1,0:T(8,128)(2,1)S(1)} %get-tuple-element.24), channel_id=1, source_target_pairs={{0,1},{2,3},{4,5},{6,7},{1,0},{3,2},{5,4},{7,6},{8,9},{10,11},{12,... | collective-permute-start | bytes 153608 | tf_op jit(solution)/shard_map/ppermute | solution.py:319

commit v4 on v3

--- a/solution.py
+++ b/solution.py
@@ -13,7 +13,7 @@
 COT_AT = C_IN * DEEP
 ONES_AT = COT_AT + 4
 BLOCKS = ONES_AT + 1
-ROWS_W2, ROWS_W1, ROWS_B, ROWS = 0, 432, 480, 512
+ROWS_W2, ROWS_W1, ROWS_B2, ROWS_B1, ROWS = 0, 432, 480, 496, 512
 
 
 def dot(a, b, dims=((1,), (0,))):
@@ -34,6 +34,10 @@
 
 def paired(v):
     return ((v + rolled(v, v.shape[1] - 1)) * 0.125).astype(BF16)
+
+
+def bias_scale():
+    return 1.0 + iota((16, 128), 0).astype(F32) * 0.0625
 
 
 def taps(v, period):
@@ -43,7 +47,7 @@
     return before, v, after
 
 
-def pack_kernel(vol_at, cot_at, w1_at, b1_at, w2_at, b2_at, across, inside, vol, cot, w1, b1, w2, b2, sems):
+def pack_kernel(vol_at, cot_at, w1_at, b1_at, w2_at, b2_at, inside, across, vol, cot, w1, b1, w2, b2, sems):
     pairs = ((vol_at, vol), (cot_at, cot), (w1_at, w1), (b1_at, b1), (w2_at, w2), (b2_at, b2))
     copies = [pltpu.make_async_copy(a, b, sems.at[i]) for i, (a, b) in enumerate(pairs)]
     for copy in copies:
@@ -120,7 +124,7 @@
     t2[:, 1152:] = bias_rows(b2[...].reshape(1, C_OUT), 4).T.astype(BF16)
 
 
-def main_kernel(vol, across, inside, cot, t1, t2, t2g, feat, grads, before, behind, p1, pre1, p2, g4x, g1):
+def main_kernel(vol, inside, across, cot, t1, t2, t2g, feat, grads, before, behind, p1, pre1, p2, g4x, g1):
     def place(first, second):
         before[...] = first[...]
         behind[...] = second[...]
@@ -159,8 +163,10 @@
     pool = jnp.where((row // 128 == col // 64) & (row % 128 == col % 64 * 2), 1.0, 0.0).astype(BF16)
     m_before = before[ONES_AT].astype(F32)[:1]
     m_behind = behind[ONES_AT].astype(F32)[:1]
+    pairs = [jnp.concatenate([pooled[r], pooled[r + 2]], axis=1) for r in range(6)]
+    chosen = dot(jnp.concatenate(pairs, axis=0), pool)
     for r in range(6):
-        act = dot(jnp.concatenate([pooled[r], pooled[r + 2]], axis=1), pool)
+        act = chosen[r * 128 : (r + 1) * 128]
         if r < 2:
             act = act * jnp.where(low, m_before, 1.0)
         if r >= 4:
@@ -200,9 +206,10 @@
         for kx, tap in enumerate(reversed(taps(piece, 64))):
             g4x[kx * 256 : (kx + 1) * 256, r * 128 : (r + 1) * 128] = tap.astype(BF16)
 
-    back = dot(t2g[0:128], g4x[:, 256:512])
-    back = back + dot(t2g[128:256], g4x[:, 128:384])
-    back = back + dot(t2g[256:384], g4x[:, 0:256])
+    early = dot(t2g[128:384], g4x[:, 0:256])
+    late = dot(t2g[0:256], g4x[:, 256:512])
+    back = jnp.concatenate([early[:128, 128:] + early[128:, :128], early[128:, 128:] + late[128:, :128]], axis=1)
+    back = back + late[:128]
     one = back * 0.125
     less = 0.3 * one
     stack = jnp.concatenate([one[:, :128], one[:, 128:], less[:, :128], less[:, 128:]], axis=0)
@@ -229,8 +236,9 @@
                 total = sum(even[1:], even[0]) + rolled(sum(odd[1:], odd[0]), 64)
                 at = ROWS_W2 + ((kd * 3 + ky) * 3 + kx) * 16
                 grads[at : at + 16] = jnp.where(low, total[:16], rolled(total[16:], 64)).astype(BF16)
-    bias2 = d2[1152:1160, :128] + d2[1152:1160, 128:]
-    bias2 = bias2 + rolled(bias2, 64)
+    scale = bias_scale()
+    bias = d2[1152:1168, :128] + d2[1152:1168, 128:]
+    grads[ROWS_B2 : ROWS_B2 + 16] = ((bias + rolled(bias, 64)) * scale).astype(BF16)
 
     d1 = dot(p1[0:304, 512:1536], g1[...], ((1,), (1,)))
     body = d1[:288].reshape(36, 8, 256)
@@ -244,11 +252,9 @@
         total = jnp.where(lane // 32 == k, part, total)
     total = jnp.concatenate([total, jnp.zeros((12, 128), F32)], axis=0)
     grads[ROWS_W1 : ROWS_W1 + 48] = total.astype(BF16)
-    bias1 = d1[288:296, :128] + d1[288:296, 128:]
-    bias1 = bias1 + rolled(bias1, 64)
-    bias1 = bias1 + rolled(bias1, 32)
-    grads[ROWS_B : ROWS_B + 16] = jnp.concatenate([bias2, bias1], axis=0).astype(BF16)
-    grads[ROWS_B + 16 :] = jnp.zeros((ROWS - ROWS_B - 16, 128), BF16)
+    bias = d1[288:304, :128] + d1[288:304, 128:]
+    bias = bias + rolled(bias, 64)
+    grads[ROWS_B1 : ROWS_B1 + 16] = ((bias + rolled(bias, 32)) * scale).astype(BF16)
 
 
 def unpack_kernel(grads, w1, b1, w2, b2):
@@ -263,9 +269,11 @@
             for kx in range(3):
                 at = (kd * 3 + kx) * C_IN
                 w1[(kd * 3 + ky) * 3 + kx] = part[at : at + C_IN, :C_MID]
-    body = grads[ROWS_B : ROWS_B + 16].astype(F32)
-    b2[...] = body[:1, :C_OUT]
-    b1[...] = body[8:9, :C_MID]
+    weigh = 1.0 / (16.0 * bias_scale())
+    body = grads[ROWS_B2 : ROWS_B2 + 16].astype(F32) * weigh
+    b2[...] = jnp.sum(body, axis=0, keepdims=True)[:, :C_OUT]
+    body = grads[ROWS_B1 : ROWS_B1 + 16].astype(F32) * weigh
+    b1[...] = jnp.sum(body, axis=0, keepdims=True)[:, :C_MID]
 
 
 def call(kernel, outs, *args, scratch=(), place=pltpu.VMEM):
@@ -304,7 +312,7 @@
     w1 = jnp.transpose(w_first, (2, 3, 4, 1, 0)).reshape(27, C_IN, C_MID)
     w2 = jnp.transpose(w_second, (2, 3, 4, 1, 0)).reshape(27, C_MID, C_OUT)
     args = [pltpu.with_memory_space_constraint(a, pltpu.HBM) for a in (volume[0], cot, w1, b_first, w2, b_second)]
-    across, inside, vol, cot, w1, b1, w2, b2 = call(
+    inside, across, vol, cot, w1, b1, w2, b2 = call(
         pack_kernel,
         [((BLOCKS, 8, 128), BF16)] * 2 + [(a.shape, a.dtype) for a in args],
         *args,
@@ -313,10 +321,10 @@
     )
     space = ("x", "core")
     count = lax.axis_size(space)
+    pairs = [(i, i + 1) for i in range(0, count, 2)]
+    inside = lax.ppermute(inside, space, pairs + [(j, i) for i, j in pairs])
     pairs = [(i, i + 1) for i in range(1, count - 1, 2)]
     across = lax.ppermute(across, space, pairs + [(j, i) for i, j in pairs])
-    pairs = [(i, i + 1) for i in range(0, count, 2)]
-    inside = lax.ppermute(inside, space, pairs + [(j, i) for i, j in pairs])
     t1, t2, t2g = call(
         weights_kernel,
         [((256, 384), BF16), ((256, 1280), BF16), ((384, 768), BF16)],
@@ -325,7 +333,7 @@
     feat, grads = call(
         main_kernel,
         [((2, 2, 32, C_OUT), BF16), ((ROWS, 128), BF16)],
-        vol, across, inside, cot, t1, t2, t2g,
+        vol, inside, across, cot, t1, t2, t2g,
         scratch=[
             pltpu.VMEM((BLOCKS, 8, 128), BF16),
             pltpu.VMEM((BLOCKS, 8, 128), BF16),

time: 67.6 us -> 68.8 us (1.018)
  waiting for transfers between devices: 0.26 us -> 2.9 us
  blocking collectives: 50.8 us -> 48.4 us
  starting transfers between devices: 9.45 us -> 10.7 us
    ppermute x1, starting transfers between devices: 4.94 us -> 8.79 us  [local(): inside = lax.ppermute(inside, space, pairs + [(j, i) for i, j in pairs])]
    ppermute x1, waiting for transfers between devices: 0.01 us -> 2.89 us  [local(): across = lax.ppermute(across, space, pairs + [(j, i) for i, j in pairs])]
    ppermute x1, starting transfers between devices: 4.51 us -> 1.92 us  [local(): across = lax.ppermute(across, space, pairs + [(j, i) for i, j in pairs])]
    all_to_all x1, blocking collectives: 11.7 us -> 9.37 us  [summed_over_devices(): pieces = lax.all_to_all(grads.reshape(count, rows, 128), near, 0, 0)]
where the time goes in v4:
time: 68.8 us; the launch traced here: 68.6 us
  blocking collectives  48.4 us (70%)
  starting transfers between devices  10.7 us (16%)
  Pallas kernels  5.89 us (9%)
  waiting for transfers between devices  2.9 us (4%)
    all_to_all x1, blocking collectives, summed_over_devices(): pieces = lax.all_to_all(mine, 'z', 0, 0)  26.2 us
    all_to_all x1, blocking collectives, summed_over_devices(): return lax.all_to_all(mine, near, 0, 0).reshape(ROWS, 128)  12.8 us
    all_to_all x1, blocking collectives, summed_over_devices(): pieces = lax.all_to_all(grads.reshape(count, rows, 128), near, 0, 0)  9.37 us
    ppermute x1, starting transfers between devices, local(): inside = lax.ppermute(inside, space, pairs + [(j, i) for i, j in pairs])  8.79 us
    pallas_call x6, Pallas kernels, call(): pl.pallas_call(kernel, out_shape=[jax.ShapeDtypeStruct(s, t) for s, t in...  5.89 us
    ppermute x1, waiting for transfers between devices, local(): across = lax.ppermute(across, space, pairs + [(j, i) for i, j in pairs])  2.89 us
    ppermute x1, starting transfers between devices, local(): across = lax.ppermute(across, space, pairs + [(j, i) for i, j in pairs])  1.92 us
  transfers between devices with their start and end apart: 2, of which 1 were waited for; matrix products, arithmetic and copies ran while one was open for 0% of the time, Pallas kernels for 1%

profile of v4, /device:TPU:1, one launch (start us, length us, event | category | flops | bytes accessed | tf_op | source)
XLA Modules:
  0.0 68.6 jit_solution(9198591449956014660)
XLA Ops:
  0.6 1.1 %shard_map.101 = (bf16[25,8,128]{2,1,0:T(8,128)(2,1)S(1)}, bf16[25,8,128]{2,1,0:T(8,128)(2,1)S(1)}, bf16[4,8,8,128]{3,2,1,0:T(8,128)(2,1)S(1)}, bf16[2,2,32,64]{...) custom-call(bf16[4,8,8,128]{3,2,1,0:T(8,128)(2,1)} %bitcast.26, ...), custom_call_target="tpu_custom_call" | custom-call | tf_op jit(solution)/shard_map/pallas_call | solution.py:280
  1.7 8.8 %collective-permute-start = (bf16[25,8,128]{2,1,0:T(8,128)(2,1)S(1)}, bf16[25,8,128]{2,1,0:T(8,128)(2,1)S(1)}, u32[]{:S(2)}, u32[]{:S(2)}) collective-permute-start(bf16[25,8,128]{2,1,0:T(8,128)(2,1)S(1)} %get-tuple-element.23), channel_id=1, source_target_pairs={{0,1},{2,3},{4,5},{6,7},{1,0},{3,2},{5,4},{7,6},{8,9},{10,11},{12,... | collective-permute-start | bytes 153608 | tf_op jit(solution)/shard_map/ppermute | solution.py:325
  10.5 1.9 %collective-permute-start.1 = (bf16[25,8,128]{2,1,0:T(8,128)(2,1)S(1)}, bf16[25,8,128]{2,1,0:T(8,128)(2,1)S(1)}, u32[]{:S(2)}, u32[]{:S(2)}) collective-permute-start(bf16[25,8,128]{2,1,0:T(8,128)(2,1)S(1)} %get-tuple-element.24), channel_id=1, source_target_pairs={{1,2},{3,4},{5,6},{2,1},{4,3},{6,5},{9,10},{11,12},{13,14},{10,9},... | collective-permute-start | bytes 153608 | tf_op jit(solution)/shard_map/ppermute | solution.py:327
  12.4 0.6 shard_map.102
  13.0 0.0 collective-permute-done.inside
  13.1 2.9 %collective-permute-done.1.across = bf16[25,8,128]{2,1,0:T(8,128)(2,1)S(1)} collective-permute-done((bf16[25,8,128]{2,1,0:T(8,128)(2,1)S(1)}, bf16[25,8,128]{2,1,0:T(8,128)(2,1)S(1)}, u32[]{:S(2)}, u32[]{:S(2)}) %collective-permute-start.1) | collective-permute-done | bytes 51232 | tf_op jit(solution)/shard_map/ppermute | solution.py:327
  16.0 3.3 %shard_map.103 = (bf16[2,2,32,64]{3,2,1,0:T(8,128)(2,1)}, bf16[512,128]{1,0:T(8,128)(2,1)S(1)}) custom-call(bf16[4,8,8,128]{3,2,1,0:T(8,128)(2,1)S(1)} %get-tuple-element.22.vol, bf16[25,8,128]{2,1,0:T(8,128)(2,1)S(1)} %collective-permute-done.inside, bf16[25,8,128]{2,1,0:T(8,128)(2,1)S(1)} %collective-permute-done.1.across, ...), custom_call_target="tpu_custom_call" | custom-call | tf_op jit(solution)/shard_map/pallas_call | solution.py:280
  19.2 9.4 %all_to_all.15.pieces = bf16[32,16,128]{2,1,0:T(8,128)(2,1)S(1)} all-to-all(bf16[32,16,128]{2,1,0:T(8,128)(2,1)S(1)} %bitcast.24), channel_id=1, replica_groups=mesh['z'=16,'y'=4,'x'=4,'core'=2] {'y','x','core'}, dimensions={0} | all-to-all | bytes 262144 | tf_op jit(solution)/shard_map/all_to_all | solution.py:303
  28.6 26.2 %all_to_all.16.pieces = bf16[16,16,128]{2,1,0:T(8,128)(2,1)S(1)} all-to-all(bf16[16,16,128]{2,1,0:T(8,128)(2,1)S(1)} %shard_map.104), channel_id=1, replica_groups=mesh['z'=16,'y'=4,'x'=4,'core'=2] {'z'}, dimensions={0} | all-to-all | bytes 131072 | tf_op jit(solution)/shard_map/all_to_all | solution.py:305
  54.9 12.8 %all_to_all.17 = bf16[32,16,128]{2,1,0:T(8,128)(2,1)S(1)} all-to-all(bf16[32,16,128]{2,1,0:T(8,128)(2,1)S(1)} %shard_map.105), channel_id=1, replica_groups=mesh['z'=16,'y'=4,'x'=4,'core'=2] {'y','x','core'}, dimensions={0} | all-to-all | bytes 262144 | tf_op jit(solution)/shard_map/all_to_all | solution.py:307
  67.7 0.9 %shard_map.106 = (f32[27,4,32]{2,1,0:T(4,128)}, f32[1,32]{1,0:T(1,128)}, f32[27,32,64]{2,1,0:T(8,128)}, f32[1,64]{1,0:T(1,128)}) custom-call(bf16[512,128]{1,0:T(8,128)(2,1)S(1)} %bitcast.23), custom_call_target="tpu_custom_call" | custom-call | tf_op jit(solution)/shard_map/pallas_call | solution.py:280
  (2 shorter events, 0.1 us)
Async XLA Ops:
  1.7 11.3 %collective-permute-start = (bf16[25,8,128]{2,1,0:T(8,128)(2,1)S(1)}, bf16[25,8,128]{2,1,0:T(8,128)(2,1)S(1)}, u32[]{:S(2)}, u32[]{:S(2)}) collective-permute-start(bf16[25,8,128]{2,1,0:T(8,128)(2,1)S(1)} %get-tuple-element.23), channel_id=1, source_target_pairs={{0,1},{2,3},{4,5},{6,7},{1,0},{3,2},{5,4},{7,6},{8,9},{10,11},{12,... | collective-permute-start | bytes 153608 | tf_op jit(solution)/shard_map/ppermute | solution.py:325
  10.5 5.4 %collective-permute-start.1 = (bf16[25,8,128]{2,1,0:T(8,128)(2,1)S(1)}, bf16[25,8,128]{2,1,0:T(8,128)(2,1)S(1)}, u32[]{:S(2)}, u32[]{:S(2)}) collective-permute-start(bf16[25,8,128]{2,1,0:T(8,128)(2,1)S(1)} %get-tuple-element.24), channel_id=1, source_target_pairs={{1,2},{3,4},{5,6},{2,1},{4,3},{6,5},{9,10},{11,12},{13,14},{10,9},... | collective-permute-start | bytes 153608 | tf_op jit(solution)/shard_map/ppermute | solution.py:327

commit v5 on v4

--- a/solution.py
+++ b/solution.py
@@ -47,7 +47,7 @@
     return before, v, after
 
 
-def pack_kernel(vol_at, cot_at, w1_at, b1_at, w2_at, b2_at, inside, across, vol, cot, w1, b1, w2, b2, sems):
+def pack_kernel(vol_at, cot_at, w1_at, b1_at, w2_at, b2_at, across, inside, vol, cot, w1, b1, w2, b2, sems):
     pairs = ((vol_at, vol), (cot_at, cot), (w1_at, w1), (b1_at, b1), (w2_at, w2), (b2_at, b2))
     copies = [pltpu.make_async_copy(a, b, sems.at[i]) for i, (a, b) in enumerate(pairs)]
     for copy in copies:
@@ -124,7 +124,7 @@
     t2[:, 1152:] = bias_rows(b2[...].reshape(1, C_OUT), 4).T.astype(BF16)
 
 
-def main_kernel(vol, inside, across, cot, t1, t2, t2g, feat, grads, before, behind, p1, pre1, p2, g4x, g1):
+def main_kernel(vol, across, inside, cot, t1, t2, t2g, feat, grads, before, behind, p1, pre1, p2, g4x, g1):
     def place(first, second):
         before[...] = first[...]
         behind[...] = second[...]
@@ -296,15 +296,22 @@
         out[i] = total
 
 
+def rounded(count, first):
+    return [[(first + i) % count for i in range(count)]]
+
+
 def summed_over_devices(grads):
     near = ("y", "x", "core")
-    count, far = lax.axis_size(near), lax.axis_size("z")
+    y, x, core = (lax.axis_size(axis) for axis in near)
+    count, far = y * x * core, lax.axis_size("z")
+    plane = rounded(count, (y // 2 * x + x // 2) * core)
+    line = rounded(far, far // 2)
     rows = ROWS // count
-    pieces = lax.all_to_all(grads.reshape(count, rows, 128), near, 0, 0)
+    pieces = lax.all_to_all(grads.reshape(count, rows, 128), near, 0, 0, axis_index_groups=plane)
     (mine,) = call(sum_kernel, [((far, rows, 128), BF16)], pieces)
-    pieces = lax.all_to_all(mine, "z", 0, 0)
+    pieces = lax.all_to_all(mine, "z", 0, 0, axis_index_groups=line)
     (mine,) = call(sum_kernel, [((count, rows, 128), BF16)], pieces)
-    return lax.all_to_all(mine, near, 0, 0).reshape(ROWS, 128)
+    return lax.all_to_all(mine, near, 0, 0, axis_index_groups=plane).reshape(ROWS, 128)
 
 
 def local(volume, w_first, b_first, w_second, b_second, cotangent):
@@ -312,7 +319,7 @@
     w1 = jnp.transpose(w_first, (2, 3, 4, 1, 0)).reshape(27, C_IN, C_MID)
     w2 = jnp.transpose(w_second, (2, 3, 4, 1, 0)).reshape(27, C_MID, C_OUT)
     args = [pltpu.with_memory_space_constraint(a, pltpu.HBM) for a in (volume[0], cot, w1, b_first, w2, b_second)]
-    inside, across, vol, cot, w1, b1, w2, b2 = call(
+    across, inside, vol, cot, w1, b1, w2, b2 = call(
         pack_kernel,
         [((BLOCKS, 8, 128), BF16)] * 2 + [(a.shape, a.dtype) for a in args],
         *args,
@@ -333,7 +340,7 @@
     feat, grads = call(
         main_kernel,
         [((2, 2, 32, C_OUT), BF16), ((ROWS, 128), BF16)],
-        vol, inside, across, cot, t1, t2, t2g,
+        vol, across, inside, cot, t1, t2, t2g,
         scratch=[
             pltpu.VMEM((BLOCKS, 8, 128), BF16),
             pltpu.VMEM((BLOCKS, 8, 128), BF16),

time: 68.8 us -> 58.1 us (0.84)
  blocking collectives: 48.4 us -> 41.5 us
  waiting for transfers between devices: 2.9 us -> 0.26 us
  starting transfers between devices: 10.7 us -> 9.45 us
    all_to_all x3, blocking collectives: 48.4 us -> 41.5 us  [the longest x1 20.1 us: summed_over_devices(): pieces = lax.all_to_all(mine, 'z', 0, 0, axis_index_groups=line)]
    ppermute x1, starting transfers between devices: 8.79 us -> 4.94 us  [local(): inside = lax.ppermute(inside, space, pairs + [(j, i) for i, j in pairs])]
    ppermute x1, waiting for transfers between devices: 2.89 us -> 0.01 us  [local(): across = lax.ppermute(across, space, pairs + [(j, i) for i, j in pairs])]
    ppermute x1, starting transfers between devices: 1.92 us -> 4.51 us  [local(): across = lax.ppermute(across, space, pairs + [(j, i) for i, j in pairs])]
where the time goes in v5:
time: 58.1 us; the launch traced here: 57.8 us
  blocking collectives  41.5 us (71%)
  starting transfers between devices  9.45 us (16%)
  Pallas kernels  5.9 us (10%)
  between operations  0.68 us (1%)
    all_to_all x1, blocking collectives, summed_over_devices(): pieces = lax.all_to_all(mine, 'z', 0, 0, axis_index_groups=line)  20.1 us
    all_to_all x1, blocking collectives, summed_over_devices(): lax.all_to_all(mine, near, 0, 0, axis_index_groups=plane).reshape(ROWS, 128)  11.6 us
    all_to_all x1, blocking collectives, summed_over_devices(): lax.all_to_all(grads.reshape(count, rows, 128), near, 0, 0, axis_index_gr...  9.89 us
    pallas_call x6, Pallas kernels, call(): pl.pallas_call(kernel, out_shape=[jax.ShapeDtypeStruct(s, t) for s, t in...  5.9 us
    ppermute x1, starting transfers between devices, local(): inside = lax.ppermute(inside, space, pairs + [(j, i) for i, j in pairs])  4.94 us
    ppermute x1, starting transfers between devices, local(): across = lax.ppermute(across, space, pairs + [(j, i) for i, j in pairs])  4.51 us
  transfers between devices with their start and end apart: 2, of which 1 were waited for; matrix products, arithmetic and copies ran while one was open for 0% of the time, Pallas kernels for 1%

profile of v5, /device:TPU:1, one launch (start us, length us, event | category | flops | bytes accessed | tf_op | source)
XLA Modules:
  0.0 57.8 jit_solution(4937559789953466078)
XLA Ops:
  0.6 1.1 %shard_map.101 = (bf16[25,8,128]{2,1,0:T(8,128)(2,1)S(1)}, bf16[25,8,128]{2,1,0:T(8,128)(2,1)S(1)}, bf16[4,8,8,128]{3,2,1,0:T(8,128)(2,1)S(1)}, bf16[2,2,32,64]{...) custom-call(bf16[4,8,8,128]{3,2,1,0:T(8,128)(2,1)} %bitcast.26, ...), custom_call_target="tpu_custom_call" | custom-call | tf_op jit(solution)/shard_map/pallas_call | solution.py:280
  1.7 4.5 %collective-permute-start = (bf16[25,8,128]{2,1,0:T(8,128)(2,1)S(1)}, bf16[25,8,128]{2,1,0:T(8,128)(2,1)S(1)}, u32[]{:S(2)}, u32[]{:S(2)}) collective-permute-start(bf16[25,8,128]{2,1,0:T(8,128)(2,1)S(1)} %get-tuple-element.23), channel_id=1, source_target_pairs={{1,2},{3,4},{5,6},{2,1},{4,3},{6,5},{9,10},{11,12},{13,14},{10,9},... | collective-permute-start | bytes 153608 | tf_op jit(solution)/shard_map/ppermute | solution.py:334
  6.2 4.9 %collective-permute-start.1 = (bf16[25,8,128]{2,1,0:T(8,128)(2,1)S(1)}, bf16[25,8,128]{2,1,0:T(8,128)(2,1)S(1)}, u32[]{:S(2)}, u32[]{:S(2)}) collective-permute-start(bf16[25,8,128]{2,1,0:T(8,128)(2,1)S(1)} %get-tuple-element.24), channel_id=1, source_target_pairs={{0,1},{2,3},{4,5},{6,7},{1,0},{3,2},{5,4},{7,6},{8,9},{10,11},{12,... | collective-permute-start | bytes 153608 | tf_op jit(solution)/shard_map/ppermute | solution.py:332
  11.2 0.6 %shard_map.102 = (bf16[256,384]{1,0:T(8,128)(2,1)S(1)}, bf16[256,1280]{1,0:T(8,128)(2,1)S(1)}, bf16[384,768]{1,0:T(8,128)(2,1)S(1)}) custom-call(bf16[27,4,32]{2,1,0:T(4,128)(2,1)S(1)} %get-tuple-element.26.w1, f32[32]{0:T(128)S(1)} %get-tuple-element.27.b1, bf16[27,32,64]{2,1,0:T(8,128)(2,1)S(1)} %get-tuple-element.28.w2, f32[64]{0:T(128)S(1)} %get-tuple-element.29.b2), custom_call_target="tpu_custom_call" | custom-call | tf_op jit(solution)/shard_map/pallas_call | solution.py:280
  11.8 0.0 collective-permute-done.across
  11.8 0.3 collective-permute-done.1.inside
  12.1 3.3 %shard_map.103 = (bf16[2,2,32,64]{3,2,1,0:T(8,128)(2,1)}, bf16[512,128]{1,0:T(8,128)(2,1)S(1)}) custom-call(bf16[4,8,8,128]{3,2,1,0:T(8,128)(2,1)S(1)} %get-tuple-element.22.vol, bf16[25,8,128]{2,1,0:T(8,128)(2,1)S(1)} %collective-permute-done.across, bf16[25,8,128]{2,1,0:T(8,128)(2,1)S(1)} %collective-permute-done.1.inside, ...), custom_call_target="tpu_custom_call" | custom-call | tf_op jit(solution)/shard_map/pallas_call | solution.py:280
  15.3 9.9 %all_to_all.15.pieces = bf16[32,16,128]{2,1,0:T(8,128)(2,1)S(1)} all-to-all(bf16[32,16,128]{2,1,0:T(8,128)(2,1)S(1)} %bitcast.24), channel_id=1, replica_groups={{20,21,22,23,24,25,26,27,28,29,30,31,0,1,2,3,4,5,6,7,8,9,10,11,12,13,14..., dimensions={0} | all-to-all | bytes 262144 | tf_op jit(solution)/shard_map/all_to_all | solution.py:310
  25.3 20.1 %all_to_all.16.pieces = bf16[16,16,128]{2,1,0:T(8,128)(2,1)S(1)} all-to-all(bf16[16,16,128]{2,1,0:T(8,128)(2,1)S(1)} %shard_map.104), channel_id=1, replica_groups={{256,288,320,352,384,416,448,480,0,32,64,96,128,160,192,224},{257,289,3..., dimensions={0} | all-to-all | bytes 131072 | tf_op jit(solution)/shard_map/all_to_all | solution.py:312
  45.4 11.6 %all_to_all.17 = bf16[32,16,128]{2,1,0:T(8,128)(2,1)S(1)} all-to-all(bf16[32,16,128]{2,1,0:T(8,128)(2,1)S(1)} %shard_map.105), channel_id=1, replica_groups={{20,21,22,23,24,25,26,27,28,29,30,31,0,1,2,3,4,5,6,7,8,9,10,11,12,13,14..., dimensions={0} | all-to-all | bytes 262144 | tf_op jit(solution)/shard_map/all_to_all | solution.py:314
  57.0 0.9 %shard_map.106 = (f32[27,4,32]{2,1,0:T(4,128)}, f32[1,32]{1,0:T(1,128)}, f32[27,32,64]{2,1,0:T(8,128)}, f32[1,64]{1,0:T(1,128)}) custom-call(bf16[512,128]{1,0:T(8,128)(2,1)S(1)} %bitcast.23), custom_call_target="tpu_custom_call" | custom-call | tf_op jit(solution)/shard_map/pallas_call | solution.py:280
  (2 shorter events, 0.1 us)
Async XLA Ops:
  1.7 10.1 %collective-permute-start = (bf16[25,8,128]{2,1,0:T(8,128)(2,1)S(1)}, bf16[25,8,128]{2,1,0:T(8,128)(2,1)S(1)}, u32[]{:S(2)}, u32[]{:S(2)}) collective-permute-start(bf16[25,8,128]{2,1,0:T(8,128)(2,1)S(1)} %get-tuple-element.23), channel_id=1, source_target_pairs={{1,2},{3,4},{5,6},{2,1},{4,3},{6,5},{9,10},{11,12},{13,14},{10,9},... | collective-permute-start | bytes 153608 | tf_op jit(solution)/shard_map/ppermute | solution.py:334
  6.2 5.8 %collective-permute-start.1 = (bf16[25,8,128]{2,1,0:T(8,128)(2,1)S(1)}, bf16[25,8,128]{2,1,0:T(8,128)(2,1)S(1)}, u32[]{:S(2)}, u32[]{:S(2)}) collective-permute-start(bf16[25,8,128]{2,1,0:T(8,128)(2,1)S(1)} %get-tuple-element.24), channel_id=1, source_target_pairs={{0,1},{2,3},{4,5},{6,7},{1,0},{3,2},{5,4},{7,6},{8,9},{10,11},{12,... | collective-permute-start | bytes 153608 | tf_op jit(solution)/shard_map/ppermute | solution.py:332

commit v6 on v5

--- a/solution.py
+++ b/solution.py
@@ -130,8 +130,8 @@
         behind[...] = second[...]
 
     core = lax.axis_index("core")
-    pl.when(core == 0)(lambda: place(across, inside))
-    pl.when(core == 1)(lambda: place(inside, across))
+    pl.when(core == 0)(lambda: place(across, inside.at[1]))
+    pl.when(core == 1)(lambda: place(inside.at[0], across))
     lane = iota((1, 128), 1)
     low = lane < 64
 
@@ -300,12 +300,16 @@
     return [[(first + i) % count for i in range(count)]]
 
 
+def farthest(count, first):
+    return [sorted(range(count), key=lambda i: (i != first, -min((i - first) % count, (first - i) % count)))]
+
+
 def summed_over_devices(grads):
     near = ("y", "x", "core")
     y, x, core = (lax.axis_size(axis) for axis in near)
     count, far = y * x * core, lax.axis_size("z")
-    plane = rounded(count, (y // 2 * x + x // 2) * core)
-    line = rounded(far, far // 2)
+    plane = rounded(count, (y // 2 * x + x // 2) * core + 1)
+    line = farthest(far, far // 2)
     rows = ROWS // count
     pieces = lax.all_to_all(grads.reshape(count, rows, 128), near, 0, 0, axis_index_groups=plane)
     (mine,) = call(sum_kernel, [((far, rows, 128), BF16)], pieces)
@@ -328,10 +332,9 @@
     )
     space = ("x", "core")
     count = lax.axis_size(space)
-    pairs = [(i, i + 1) for i in range(0, count, 2)]
-    inside = lax.ppermute(inside, space, pairs + [(j, i) for i, j in pairs])
     pairs = [(i, i + 1) for i in range(1, count - 1, 2)]
     across = lax.ppermute(across, space, pairs + [(j, i) for i, j in pairs])
+    inside = lax.all_gather(inside, "core")
     t1, t2, t2g = call(
         weights_kernel,
         [((256, 384), BF16), ((256, 1280), BF16), ((384, 768), BF16)],

time: 58.1 us -> 57.2 us (0.985)
  starting transfers between devices: 9.45 us -> 4.51 us
  blocking collectives: 41.5 us -> 45.9 us
    ppermute x1 -> x0, starting transfers between devices: 4.94 us -> none  [local(): inside = lax.ppermute(inside, space, pairs + [(j, i) for i, j in pairs])]
    all_gather x0 -> x1, blocking collectives: none -> 4.56 us  [local(): inside = lax.all_gather(inside, 'core')]
    all_to_all x1, blocking collectives: 11.6 us -> 12.2 us  [summed_over_devices(): lax.all_to_all(mine, near, 0, 0, axis_index_groups=plane).reshape(ROWS, 128)]
  transfers between devices with their start and end apart: 2 -> 1, of which waited for: 1 -> 0; matrix products, arithmetic and copies ran while one was open for 0% -> 0% of each run, Pallas kernels for 1% -> 1%
where the time goes in v6:
time: 57.2 us; the launch traced here: 56.9 us
  blocking collectives  45.9 us (80%)
  Pallas kernels  5.89 us (10%)
  starting transfers between devices  4.51 us (8%)
  between operations  0.67 us (1%)
    all_to_all x1, blocking collectives, summed_over_devices(): pieces = lax.all_to_all(mine, 'z', 0, 0, axis_index_groups=line)  19.5 us
    all_to_all x1, blocking collectives, summed_over_devices(): lax.all_to_all(mine, near, 0, 0, axis_index_groups=plane).reshape(ROWS, 128)  12.2 us
    all_to_all x1, blocking collectives, summed_over_devices(): lax.all_to_all(grads.reshape(count, rows, 128), near, 0, 0, axis_index_gr...  9.61 us
    pallas_call x6, Pallas kernels, call(): pl.pallas_call(kernel, out_shape=[jax.ShapeDtypeStruct(s, t) for s, t in...  5.89 us
    all_gather x1, blocking collectives, local(): inside = lax.all_gather(inside, 'core')  4.56 us
    ppermute x1, starting transfers between devices, local(): across = lax.ppermute(across, space, pairs + [(j, i) for i, j in pairs])  4.51 us
  transfers between devices with their start and end apart: 1, of which 0 were waited for; matrix products, arithmetic and copies ran while one was open for 0% of the time, Pallas kernels for 1%

profile of v6, /device:TPU:1, one launch (start us, length us, event | category | flops | bytes accessed | tf_op | source)
XLA Modules:
  0.0 56.9 jit_solution(764431022934622248)
XLA Ops:
  0.6 1.1 %shard_map.101 = (bf16[25,8,128]{2,1,0:T(8,128)(2,1)S(1)}, bf16[25,8,128]{2,1,0:T(8,128)(2,1)S(1)}, bf16[4,8,8,128]{3,2,1,0:T(8,128)(2,1)S(1)}, bf16[2,2,32,64]{...) custom-call(bf16[4,8,8,128]{3,2,1,0:T(8,128)(2,1)} %bitcast.28, ...), custom_call_target="tpu_custom_call" | custom-call | tf_op jit(solution)/shard_map/pallas_call | solution.py:280
  1.7 4.5 %collective-permute-start = (bf16[25,8,128]{2,1,0:T(8,128)(2,1)S(1)}, bf16[25,8,128]{2,1,0:T(8,128)(2,1)S(1)}, u32[]{:S(2)}, u32[]{:S(2)}) collective-permute-start(bf16[25,8,128]{2,1,0:T(8,128)(2,1)S(1)} %get-tuple-element.23), channel_id=1, source_target_pairs={{1,2},{3,4},{5,6},{2,1},{4,3},{6,5},{9,10},{11,12},{13,14},{10,9},... | collective-permute-start | bytes 153608 | tf_op jit(solution)/shard_map/ppermute | solution.py:336
  6.2 0.6 %shard_map.102 = (bf16[256,384]{1,0:T(8,128)(2,1)S(1)}, bf16[256,1280]{1,0:T(8,128)(2,1)S(1)}, bf16[384,768]{1,0:T(8,128)(2,1)S(1)}) custom-call(bf16[27,4,32]{2,1,0:T(4,128)(2,1)S(1)} %get-tuple-element.26.w1, f32[32]{0:T(128)S(1)} %get-tuple-element.27.b1, bf16[27,32,64]{2,1,0:T(8,128)(2,1)S(1)} %get-tuple-element.28.w2, f32[64]{0:T(128)S(1)} %get-tuple-element.29.b2), custom_call_target="tpu_custom_call" | custom-call | tf_op jit(solution)/shard_map/pallas_call | solution.py:280
  6.8 4.6 %all-gather = bf16[50,8,128]{2,1,0:T(8,128)(2,1)S(1)} all-gather(bf16[25,8,128]{2,1,0:T(8,128)(2,1)S(1)} %get-tuple-element.24), channel_id=2, replica_groups=mesh['z'=16,'y'=4,'x'=4,'core'=2] {'core'}, dimensions={0}, use_global_device_ids=true | all-gather | bytes 153600 | tf_op jit(solution)/shard_map/all_gather | solution.py:337
  11.4 0.0 collective-permute-done.across
  11.4 3.3 %shard_map.103 = (bf16[2,2,32,64]{3,2,1,0:T(8,128)(2,1)}, bf16[512,128]{1,0:T(8,128)(2,1)S(1)}) custom-call(bf16[4,8,8,128]{3,2,1,0:T(8,128)(2,1)S(1)} %get-tuple-element.22.vol, bf16[25,8,128]{2,1,0:T(8,128)(2,1)S(1)} %collective-permute-done.across, bf16[2,25,8,128]{3,2,1,0:T(8,128)(2,1)S(1)} %bitcast.25, ...), custom_call_target="tpu_custom_call" | custom-call | tf_op jit(solution)/shard_map/pallas_call | solution.py:280
  14.7 9.6 %all_to_all.15.pieces = bf16[32,16,128]{2,1,0:T(8,128)(2,1)S(1)} all-to-all(bf16[32,16,128]{2,1,0:T(8,128)(2,1)S(1)} %bitcast.26), channel_id=1, replica_groups={{21,22,23,24,25,26,27,28,29,30,31,0,1,2,3,4,5,6,7,8,9,10,11,12,13,14,15..., dimensions={0} | all-to-all | bytes 262144 | tf_op jit(solution)/shard_map/all_to_all | solution.py:314
  24.3 19.5 %all_to_all.16.pieces = bf16[16,16,128]{2,1,0:T(8,128)(2,1)S(1)} all-to-all(bf16[16,16,128]{2,1,0:T(8,128)(2,1)S(1)} %shard_map.104), channel_id=1, replica_groups={{256,0,32,480,64,448,96,416,128,384,160,352,192,320,224,288},{257,1,33,..., dimensions={0} | all-to-all | bytes 131072 | tf_op jit(solution)/shard_map/all_to_all | solution.py:316
  43.9 12.2 %all_to_all.17 = bf16[32,16,128]{2,1,0:T(8,128)(2,1)S(1)} all-to-all(bf16[32,16,128]{2,1,0:T(8,128)(2,1)S(1)} %shard_map.105), channel_id=1, replica_groups={{21,22,23,24,25,26,27,28,29,30,31,0,1,2,3,4,5,6,7,8,9,10,11,12,13,14,15..., dimensions={0} | all-to-all | bytes 262144 | tf_op jit(solution)/shard_map/all_to_all | solution.py:318
  56.1 0.9 %shard_map.106 = (f32[27,4,32]{2,1,0:T(4,128)}, f32[1,32]{1,0:T(1,128)}, f32[27,32,64]{2,1,0:T(8,128)}, f32[1,64]{1,0:T(1,128)}) custom-call(bf16[512,128]{1,0:T(8,128)(2,1)S(1)} %bitcast.24), custom_call_target="tpu_custom_call" | custom-call | tf_op jit(solution)/shard_map/pallas_call | solution.py:280
  (2 shorter events, 0.1 us)
Async XLA Ops:
  1.7 9.7 %collective-permute-start = (bf16[25,8,128]{2,1,0:T(8,128)(2,1)S(1)}, bf16[25,8,128]{2,1,0:T(8,128)(2,1)S(1)}, u32[]{:S(2)}, u32[]{:S(2)}) collective-permute-start(bf16[25,8,128]{2,1,0:T(8,128)(2,1)S(1)} %get-tuple-element.23), channel_id=1, source_target_pairs={{1,2},{3,4},{5,6},{2,1},{4,3},{6,5},{9,10},{11,12},{13,14},{10,9},... | collective-permute-start | bytes 153608 | tf_op jit(solution)/shard_map/ppermute | solution.py:336

commit v7 on v6

--- a/solution.py
+++ b/solution.py
@@ -101,7 +101,7 @@
                     halves.append(total)
                 blocks.append(jnp.concatenate(halves, axis=1))
     body = jnp.concatenate(blocks + [bias_rows(b1[...].reshape(1, C_MID), 8)[:96]], axis=0)
-    t1[...] = body.T.astype(BF16)
+    t1[...] = body.astype(BF16).T
     nothing = jnp.zeros((C_MID, C_OUT), F32)
     for kd in range(3):
         for kx in range(3):
@@ -120,7 +120,7 @@
             )
             t2g[kd * 128 : (kd + 1) * 128, kx * 256 : (kx + 1) * 256] = block.astype(BF16)
             at = (kd * 3 + kx) * 128
-            t2[:, at : at + 128] = block.T.astype(BF16)
+            t2[:, at : at + 128] = block.astype(BF16).T
     t2[:, 1152:] = bias_rows(b2[...].reshape(1, C_OUT), 4).T.astype(BF16)
 
 
@@ -180,16 +180,6 @@
 
     pre2 = dot(t2[...], p2[...])
 
-    act = leaky(pre2[:, 128:384]).reshape(2, 2, C_OUT, 256)
-    act = act[:, 0] + act[:, 1]
-    act = act[:, :, :128] + act[:, :, 128:]
-    row, col = iota((64, 128), 0), iota((64, 128), 1)
-    pool = jnp.where((row // 32 == col // 64) & (row % 32 * 2 == col % 64), 1.0, 0.0).astype(BF16)
-    for y in range(2):
-        out = dot(pool, paired(act[y]), ((1,), (1,)))
-        for d in range(2):
-            feat[d, y] = out[d * 32 : (d + 1) * 32].astype(BF16)
-
     pieces = [before[COT_AT:ONES_AT].astype(F32).reshape(32, 128)]
     for d in range(2):
         pieces.append(jnp.concatenate([cot[d, 0].astype(F32), cot[d, 1].astype(F32)], axis=1))
@@ -205,6 +195,16 @@
         piece = grad[:, r * 128 : (r + 1) * 128].astype(F32)
         for kx, tap in enumerate(reversed(taps(piece, 64))):
             g4x[kx * 256 : (kx + 1) * 256, r * 128 : (r + 1) * 128] = tap.astype(BF16)
+
+    act = leaky(pre2[:, 128:384]).reshape(2, 2, C_OUT, 256)
+    act = act[:, 0] + act[:, 1]
+    act = act[:, :, :128] + act[:, :, 128:]
+    row, col = iota((64, 128), 0), iota((64, 128), 1)
+    pool = jnp.where((row // 32 == col // 64) & (row % 32 * 2 == col % 64), 1.0, 0.0).astype(BF16)
+    for y in range(2):
+        out = dot(pool, paired(act[y]), ((1,), (1,)))
+        for d in range(2):
+            feat[d, y] = out[d * 32 : (d + 1) * 32].astype(BF16)
 
     early = dot(t2g[128:384], g4x[:, 0:256])
     late = dot(t2g[0:256], g4x[:, 256:512])
@@ -309,7 +309,7 @@
     y, x, core = (lax.axis_size(axis) for axis in near)
     count, far = y * x * core, lax.axis_size("z")
     plane = rounded(count, (y // 2 * x + x // 2) * core + 1)
-    line = farthest(far, far // 2)
+    line = farthest(far, far // 2 + 1)
     rows = ROWS // count
     pieces = lax.all_to_all(grads.reshape(count, rows, 128), near, 0, 0, axis_index_groups=plane)
     (mine,) = call(sum_kernel, [((far, rows, 128), BF16)], pieces)

time: 57.2 us -> 56.9 us (level)
  no operation moved by 1% of the time
where the time goes in v7:
time: 56.9 us; the launch traced here: 56.7 us
  blocking collectives  45.9 us (81%)
  Pallas kernels  5.56 us (10%)
  starting transfers between devices  4.51 us (8%)
  between operations  0.67 us (1%)
    all_to_all x1, blocking collectives, summed_over_devices(): pieces = lax.all_to_all(mine, 'z', 0, 0, axis_index_groups=line)  19.7 us
    all_to_all x1, blocking collectives, summed_over_devices(): lax.all_to_all(mine, near, 0, 0, axis_index_groups=plane).reshape(ROWS, 128)  12.1 us
    all_to_all x1, blocking collectives, summed_over_devices(): lax.all_to_all(grads.reshape(count, rows, 128), near, 0, 0, axis_index_gr...  9.61 us
    pallas_call x6, Pallas kernels, call(): pl.pallas_call(kernel, out_shape=[jax.ShapeDtypeStruct(s, t) for s, t in...  5.56 us
    all_gather x1, blocking collectives, local(): inside = lax.all_gather(inside, 'core')  4.56 us
    ppermute x1, starting transfers between devices, local(): across = lax.ppermute(across, space, pairs + [(j, i) for i, j in pairs])  4.51 us
  transfers between devices with their start and end apart: 1, of which 0 were waited for; matrix products, arithmetic and copies ran while one was open for 0% of the time, Pallas kernels for 1%

profile of v7, /device:TPU:1, one launch (start us, length us, event | category | flops | bytes accessed | tf_op | source)
XLA Modules:
  0.0 56.7 jit_solution(6913789759013902428)
XLA Ops:
  0.6 1.1 %shard_map.101 = (bf16[25,8,128]{2,1,0:T(8,128)(2,1)S(1)}, bf16[25,8,128]{2,1,0:T(8,128)(2,1)S(1)}, bf16[4,8,8,128]{3,2,1,0:T(8,128)(2,1)S(1)}, bf16[2,2,32,64]{...) custom-call(bf16[4,8,8,128]{3,2,1,0:T(8,128)(2,1)} %bitcast.28, ...), custom_call_target="tpu_custom_call" | custom-call | tf_op jit(solution)/shard_map/pallas_call | solution.py:280
  1.7 4.5 %collective-permute-start = (bf16[25,8,128]{2,1,0:T(8,128)(2,1)S(1)}, bf16[25,8,128]{2,1,0:T(8,128)(2,1)S(1)}, u32[]{:S(2)}, u32[]{:S(2)}) collective-permute-start(bf16[25,8,128]{2,1,0:T(8,128)(2,1)S(1)} %get-tuple-element.23), channel_id=1, source_target_pairs={{1,2},{3,4},{5,6},{2,1},{4,3},{6,5},{9,10},{11,12},{13,14},{10,9},... | collective-permute-start | bytes 153608 | tf_op jit(solution)/shard_map/ppermute | solution.py:336
  6.2 0.5 shard_map.102
  6.7 4.6 %all-gather = bf16[50,8,128]{2,1,0:T(8,128)(2,1)S(1)} all-gather(bf16[25,8,128]{2,1,0:T(8,128)(2,1)S(1)} %get-tuple-element.24), channel_id=2, replica_groups=mesh['z'=16,'y'=4,'x'=4,'core'=2] {'core'}, dimensions={0}, use_global_device_ids=true | all-gather | bytes 153600 | tf_op jit(solution)/shard_map/all_gather | solution.py:337
  11.3 0.0 collective-permute-done.across
  11.3 3.0 %shard_map.103 = (bf16[2,2,32,64]{3,2,1,0:T(8,128)(2,1)}, bf16[512,128]{1,0:T(8,128)(2,1)S(1)}) custom-call(bf16[4,8,8,128]{3,2,1,0:T(8,128)(2,1)S(1)} %get-tuple-element.22.vol, bf16[25,8,128]{2,1,0:T(8,128)(2,1)S(1)} %collective-permute-done.across, bf16[2,25,8,128]{3,2,1,0:T(8,128)(2,1)S(1)} %bitcast.25, ...), custom_call_target="tpu_custom_call" | custom-call | tf_op jit(solution)/shard_map/pallas_call | solution.py:280
  14.4 9.6 %all_to_all.15.pieces = bf16[32,16,128]{2,1,0:T(8,128)(2,1)S(1)} all-to-all(bf16[32,16,128]{2,1,0:T(8,128)(2,1)S(1)} %bitcast.26), channel_id=1, replica_groups={{21,22,23,24,25,26,27,28,29,30,31,0,1,2,3,4,5,6,7,8,9,10,11,12,13,14,15..., dimensions={0} | all-to-all | bytes 262144 | tf_op jit(solution)/shard_map/all_to_all | solution.py:314
  24.0 19.7 %all_to_all.16.pieces = bf16[16,16,128]{2,1,0:T(8,128)(2,1)S(1)} all-to-all(bf16[16,16,128]{2,1,0:T(8,128)(2,1)S(1)} %shard_map.104), channel_id=1, replica_groups={{288,32,0,64,96,480,128,448,160,416,192,384,224,352,256,320},{289,33,1,..., dimensions={0} | all-to-all | bytes 131072 | tf_op jit(solution)/shard_map/all_to_all | solution.py:316
  43.7 12.1 %all_to_all.17 = bf16[32,16,128]{2,1,0:T(8,128)(2,1)S(1)} all-to-all(bf16[32,16,128]{2,1,0:T(8,128)(2,1)S(1)} %shard_map.105), channel_id=1, replica_groups={{21,22,23,24,25,26,27,28,29,30,31,0,1,2,3,4,5,6,7,8,9,10,11,12,13,14,15..., dimensions={0} | all-to-all | bytes 262144 | tf_op jit(solution)/shard_map/all_to_all | solution.py:318
  55.8 0.9 %shard_map.106 = (f32[27,4,32]{2,1,0:T(4,128)}, f32[1,32]{1,0:T(1,128)}, f32[27,32,64]{2,1,0:T(8,128)}, f32[1,64]{1,0:T(1,128)}) custom-call(bf16[512,128]{1,0:T(8,128)(2,1)S(1)} %bitcast.24), custom_call_target="tpu_custom_call" | custom-call | tf_op jit(solution)/shard_map/pallas_call | solution.py:280
  (2 shorter events, 0.1 us)
Async XLA Ops:
  1.7 9.6 %collective-permute-start = (bf16[25,8,128]{2,1,0:T(8,128)(2,1)S(1)}, bf16[25,8,128]{2,1,0:T(8,128)(2,1)S(1)}, u32[]{:S(2)}, u32[]{:S(2)}) collective-permute-start(bf16[25,8,128]{2,1,0:T(8,128)(2,1)S(1)} %get-tuple-element.23), channel_id=1, source_target_pairs={{1,2},{3,4},{5,6},{2,1},{4,3},{6,5},{9,10},{11,12},{13,14},{10,9},... | collective-permute-start | bytes 153608 | tf_op jit(solution)/shard_map/ppermute | solution.py:336

commit v8 on v7

--- a/solution.py
+++ b/solution.py
@@ -102,15 +102,15 @@
                 blocks.append(jnp.concatenate(halves, axis=1))
     body = jnp.concatenate(blocks + [bias_rows(b1[...].reshape(1, C_MID), 8)[:96]], axis=0)
     t1[...] = body.astype(BF16).T
-    nothing = jnp.zeros((C_MID, C_OUT), F32)
+    nothing = jnp.zeros((C_MID, C_OUT), BF16)
     for kd in range(3):
         for kx in range(3):
-            w = [w2[(kd * 3 + ky) * 3 + kx].astype(F32) for ky in range(3)]
+            w = [w2[(kd * 3 + ky) * 3 + kx] for ky in range(3)]
             pair = {
                 a: jnp.concatenate([w[a] if a < 3 else nothing, w[a - 1] if a > 0 else nothing], axis=1)
                 for a in range(4)
             }
-            none = jnp.zeros((C_MID, 128), F32)
+            none = jnp.zeros((C_MID, 128), BF16)
             block = jnp.concatenate(
                 [
                     jnp.concatenate([pair.get(y - 2 * p + 1, none) for p in range(2)], axis=1)
@@ -118,9 +118,9 @@
                 ],
                 axis=0,
             )
-            t2g[kd * 128 : (kd + 1) * 128, kx * 256 : (kx + 1) * 256] = block.astype(BF16)
+            t2g[kd * 128 : (kd + 1) * 128, kx * 256 : (kx + 1) * 256] = block
             at = (kd * 3 + kx) * 128
-            t2[:, at : at + 128] = block.astype(BF16).T
+            t2[:, at : at + 128] = block.T
     t2[:, 1152:] = bias_rows(b2[...].reshape(1, C_OUT), 4).T.astype(BF16)
 
 

time: 56.9 us -> 56.9 us (level)
  no operation moved by 1% of the time
where the time goes in v8:
time: 56.9 us; the launch traced here: 56.7 us
  blocking collectives  45.9 us (81%)
  Pallas kernels  5.56 us (10%)
  starting transfers between devices  4.51 us (8%)
  between operations  0.67 us (1%)
    all_to_all x1, blocking collectives, summed_over_devices(): pieces = lax.all_to_all(mine, 'z', 0, 0, axis_index_groups=line)  19.7 us
    all_to_all x1, blocking collectives, summed_over_devices(): lax.all_to_all(mine, near, 0, 0, axis_index_groups=plane).reshape(ROWS, 128)  12.1 us
    all_to_all x1, blocking collectives, summed_over_devices(): lax.all_to_all(grads.reshape(count, rows, 128), near, 0, 0, axis_index_gr...  9.6 us
    pallas_call x6, Pallas kernels, call(): pl.pallas_call(kernel, out_shape=[jax.ShapeDtypeStruct(s, t) for s, t in...  5.56 us
    all_gather x1, blocking collectives, local(): inside = lax.all_gather(inside, 'core')  4.56 us
    ppermute x1, starting transfers between devices, local(): across = lax.ppermute(across, space, pairs + [(j, i) for i, j in pairs])  4.51 us
  transfers between devices with their start and end apart: 1, of which 0 were waited for; matrix products, arithmetic and copies ran while one was open for 0% of the time, Pallas kernels for 1%

profile of v8, /device:TPU:1, one launch (start us, length us, event | category | flops | bytes accessed | tf_op | source)
XLA Modules:
  0.0 56.7 jit_solution(798457441029227944)
XLA Ops:
  0.6 1.1 %shard_map.101 = (bf16[25,8,128]{2,1,0:T(8,128)(2,1)S(1)}, bf16[25,8,128]{2,1,0:T(8,128)(2,1)S(1)}, bf16[4,8,8,128]{3,2,1,0:T(8,128)(2,1)S(1)}, bf16[2,2,32,64]{...) custom-call(bf16[4,8,8,128]{3,2,1,0:T(8,128)(2,1)} %bitcast.28, ...), custom_call_target="tpu_custom_call" | custom-call | tf_op jit(solution)/shard_map/pallas_call | solution.py:280
  1.7 4.5 %collective-permute-start = (bf16[25,8,128]{2,1,0:T(8,128)(2,1)S(1)}, bf16[25,8,128]{2,1,0:T(8,128)(2,1)S(1)}, u32[]{:S(2)}, u32[]{:S(2)}) collective-permute-start(bf16[25,8,128]{2,1,0:T(8,128)(2,1)S(1)} %get-tuple-element.23), channel_id=1, source_target_pairs={{1,2},{3,4},{5,6},{2,1},{4,3},{6,5},{9,10},{11,12},{13,14},{10,9},... | collective-permute-start | bytes 153608 | tf_op jit(solution)/shard_map/ppermute | solution.py:336
  6.2 0.5 shard_map.102
  6.7 4.6 %all-gather = bf16[50,8,128]{2,1,0:T(8,128)(2,1)S(1)} all-gather(bf16[25,8,128]{2,1,0:T(8,128)(2,1)S(1)} %get-tuple-element.24), channel_id=2, replica_groups=mesh['z'=16,'y'=4,'x'=4,'core'=2] {'core'}, dimensions={0}, use_global_device_ids=true | all-gather | bytes 153600 | tf_op jit(solution)/shard_map/all_gather | solution.py:337
  11.3 0.0 collective-permute-done.across
  11.3 3.0 %shard_map.103 = (bf16[2,2,32,64]{3,2,1,0:T(8,128)(2,1)}, bf16[512,128]{1,0:T(8,128)(2,1)S(1)}) custom-call(bf16[4,8,8,128]{3,2,1,0:T(8,128)(2,1)S(1)} %get-tuple-element.22.vol, bf16[25,8,128]{2,1,0:T(8,128)(2,1)S(1)} %collective-permute-done.across, bf16[2,25,8,128]{3,2,1,0:T(8,128)(2,1)S(1)} %bitcast.25, ...), custom_call_target="tpu_custom_call" | custom-call | tf_op jit(solution)/shard_map/pallas_call | solution.py:280
  14.4 9.6 %all_to_all.15.pieces = bf16[32,16,128]{2,1,0:T(8,128)(2,1)S(1)} all-to-all(bf16[32,16,128]{2,1,0:T(8,128)(2,1)S(1)} %bitcast.26), channel_id=1, replica_groups={{21,22,23,24,25,26,27,28,29,30,31,0,1,2,3,4,5,6,7,8,9,10,11,12,13,14,15..., dimensions={0} | all-to-all | bytes 262144 | tf_op jit(solution)/shard_map/all_to_all | solution.py:314
  24.0 19.7 %all_to_all.16.pieces = bf16[16,16,128]{2,1,0:T(8,128)(2,1)S(1)} all-to-all(bf16[16,16,128]{2,1,0:T(8,128)(2,1)S(1)} %shard_map.104), channel_id=1, replica_groups={{288,32,0,64,96,480,128,448,160,416,192,384,224,352,256,320},{289,33,1,..., dimensions={0} | all-to-all | bytes 131072 | tf_op jit(solution)/shard_map/all_to_all | solution.py:316
  43.7 12.1 %all_to_all.17 = bf16[32,16,128]{2,1,0:T(8,128)(2,1)S(1)} all-to-all(bf16[32,16,128]{2,1,0:T(8,128)(2,1)S(1)} %shard_map.105), channel_id=1, replica_groups={{21,22,23,24,25,26,27,28,29,30,31,0,1,2,3,4,5,6,7,8,9,10,11,12,13,14,15..., dimensions={0} | all-to-all | bytes 262144 | tf_op jit(solution)/shard_map/all_to_all | solution.py:318
  55.8 0.9 %shard_map.106 = (f32[27,4,32]{2,1,0:T(4,128)}, f32[1,32]{1,0:T(1,128)}, f32[27,32,64]{2,1,0:T(8,128)}, f32[1,64]{1,0:T(1,128)}) custom-call(bf16[512,128]{1,0:T(8,128)(2,1)S(1)} %bitcast.24), custom_call_target="tpu_custom_call" | custom-call | tf_op jit(solution)/shard_map/pallas_call | solution.py:280
  (2 shorter events, 0.1 us)
Async XLA Ops:
  1.7 9.6 %collective-permute-start = (bf16[25,8,128]{2,1,0:T(8,128)(2,1)S(1)}, bf16[25,8,128]{2,1,0:T(8,128)(2,1)S(1)}, u32[]{:S(2)}, u32[]{:S(2)}) collective-permute-start(bf16[25,8,128]{2,1,0:T(8,128)(2,1)S(1)} %get-tuple-element.23), channel_id=1, source_target_pairs={{1,2},{3,4},{5,6},{2,1},{4,3},{6,5},{9,10},{11,12},{13,14},{10,9},... | collective-permute-start | bytes 153608 | tf_op jit(solution)/shard_map/ppermute | solution.py:336
